TPU v7x, 128 devices: a whole 4x4x4 slice. The times are simulated.
128 devices in a mesh: row: 8 (over x, y_hi), col: 16 (over z, y_lo, core).
Axes of the slice: x: 4, y: 4 (y_hi: 2, y_lo: 2; y = y_hi * 2 + y_lo), z: 4, core: 2. Of those that a mesh axis runs over, the one named last changes fastest.
Arguments:
- moment_x: bfloat16 [128, 512, 512], P('row', 'col'), may hold values from -0.25 to 0.25
- moment_s: bfloat16 [128, 512, 512], P('row', 'col'), may hold values from -0.25 to 0.25
- coeffs: bfloat16 [128, 32, 512, 512], P(('row', 'col')), may hold values from -0.125 to 0.125
- slot_con: int32 [128, 32], replicated, may hold values from 0 to 8191, as said below
- con_pos: int32 [8192], replicated, may hold values from 0 to 8191, as said below
- schur_prev: float32 [8192, 8192], P('row', 'col'), may hold values from -6 to 6
- panel_inv: float32 [256, 256], replicated, as said below
Outputs:
- updated: float32 [8192, 8192], P('row', 'col')
- panel_factor: float32 [8192, 256], P('row')
Inputs may be any that keep to these rules, and one draw needn't show every extreme that they name: Within each block the 32 slots name distinct constraints; with positions = con_pos[slot_con], slot s of every block has positions // 512 == s // 2. `con_pos`: A permutation of the 8192 constraints. `panel_inv`: upper triangular with a positive diagonal.
All inputs are finite; a program needn't handle non-finite values.
Results may differ from a plain program's by a relative error of at most 0.0003.
Values may be sent and summed in bfloat16 or wider, within the bound.
A program may use at most 192 MiB of HBM per device.

v0:
```python
import jax
import jax.numpy as jnp
from jax import lax
from jax.sharding import PartitionSpec as P

TILE = 16
PW = 256


def broadcast(value, axis, source):
    kept = jnp.where(lax.axis_index(axis) == source, value, 0).astype(value.dtype)
    return lax.psum(kept, axis)


def per_device(moment_x, moment_s, coeffs, slot_con, con_pos, schur_prev, panel_inv):
    row_count = lax.axis_size("row")
    col_count = lax.axis_size("col")
    row_index = lax.axis_index("row")
    col_index = lax.axis_index("col")
    group = col_count // row_count
    block_x, block_s = (
        lax.all_to_all(moment_x, "col", split_axis=0, concat_axis=1, tiled=True),
        lax.all_to_all(moment_s, "col", split_axis=0, concat_axis=1, tiled=True),
    )
    primal = block_x[0]
    inverse_dual = block_s[0]
    constraint_slots = coeffs[0]
    count = constraint_slots.shape[0]
    order = constraint_slots.shape[1]
    left_prod = jnp.einsum(
        "pq,nqr->npr", primal, constraint_slots, preferred_element_type=jnp.float32
    ).astype(jnp.bfloat16)
    mapped_image = jnp.einsum(
        "npr,rs->nps", left_prod, inverse_dual, preferred_element_type=jnp.float32
    ).astype(jnp.bfloat16)
    entries = lax.dot_general(
        constraint_slots.reshape(count, order * order),
        mapped_image.reshape(count, order * order),
        (((1,), (1,)), ((), ())),
        preferred_element_type=jnp.float32,
    )
    per_class = count // col_count
    grouped = entries.reshape(row_count, group, per_class, col_count, per_class)
    outgoing = jnp.transpose(grouped, (0, 3, 1, 2, 4)).reshape(
        row_count * col_count, group, per_class, per_class
    )
    arrived = lax.all_to_all(outgoing, ("row", "col"), split_axis=0, concat_axis=0, tiled=True)
    received = arrived.reshape(row_count, col_count, group, per_class, per_class)
    positions = jnp.take(con_pos, slot_con, axis=0)
    slab = schur_prev.shape[0]
    cols_dev = schur_prev.shape[1]
    row_pos = jnp.take(
        positions.reshape(row_count, col_count, row_count, group, per_class), row_index, axis=2
    )
    col_pos = jnp.take(
        positions.reshape(row_count, col_count, col_count, per_class), col_index, axis=2
    )
    local_rows = row_pos - row_index * slab
    local_cols = col_pos - col_index * cols_dev
    schur = schur_prev.at[local_rows[..., None], local_cols[:, :, None, None, :]].add(received)
    width_local = PW // col_count
    local_panel = schur[:, :width_local]
    inverse_rows = jnp.take(
        panel_inv.reshape(width_local // TILE, col_count, TILE, PW), col_index, axis=1
    ).reshape(width_local, PW)
    partial_factor = jnp.dot(local_panel, inverse_rows, precision=lax.Precision.HIGHEST)
    panel_factor = lax.psum(partial_factor, "col")
    own_rows = lax.dynamic_slice_in_dim(panel_factor, col_index % group * cols_dev, cols_dev, 0)
    column_factor = broadcast(own_rows, "row", col_index // group)
    updated = schur - lax.dot_general(
        panel_factor, column_factor, (((1,), (1,)), ((), ())), precision=lax.Precision.HIGHEST
    )
    return (updated, panel_factor)


def solution(mesh):
    placed = (
        P("row", "col", None),
        P("row", "col", None),
        P(("row", "col"), None, None, None),
        P(),
        P(),
        P("row", "col"),
        P(),
    )
    return jax.shard_map(
        per_device,
        mesh=mesh,
        in_specs=placed,
        out_specs=(P("row", "col"), P("row", None)),
        check_vma=False,
    )
```

profile of v0, /device:TPU:1, one launch (start us, length us, event | category | flops | bytes accessed | tf_op | source)
XLA Modules:
  0.0 365.8 jit_solution(12785789500533715091)
XLA Ops:
  7.2 7.9 %all-to-all-start = ((bf16[16,32,512]{2,1,0:T(8,128)(2,1)}), bf16[16,32,512]{2,1,0:T(8,128)(2,1)S(1)}, u32[]{:S(2)}, u32[]{:S(2)}) async-start(bf16[16,32,512]{2,1,0:T(8,128)(2,1)} %param.7), calls=%async_computation | async-start | bytes 1048576 | tf_op jit(solution)/shard_map/all_to_all | solution.py:22
  15.0 0.8 copy.39
  15.9 0.1 reshape.200
  16.0 23.0 %gather_fusion = s32[4096]{0:T(1024)S(1)} fusion(s32[8192]{0:T(1024)S(1)} %copy-done, s32[4096]{0:T(1024)S(1)} %broadcast_clamp_fusion), kind=kCustom, calls=%fused_computation | custom fusion | bytes 49152 | tf_op jit(solution)/shard_map/jit(_take)/gather | solution.py:49
  39.0 0.1 reshape.199
  39.1 5.7 %all-to-all-start.1 = ((bf16[16,32,512]{2,1,0:T(8,128)(2,1)}), bf16[16,32,512]{2,1,0:T(8,128)(2,1)S(1)}, u32[]{:S(2)}, u32[]{:S(2)}) async-start(bf16[16,32,512]{2,1,0:T(8,128)(2,1)} %param.8), calls=%async_computation.1 | async-start | bytes 1048576 | tf_op jit(solution)/shard_map/all_to_all | solution.py:23
  44.9 0.1 select_n.96
  45.0 0.1 select_n.92
  45.1 18.5 %copy.56 = bf16[4,8,512,512]{3,1,2,0:T(8,128)(2,1)} copy(bf16[4,8,512,512]{3,2,1,0:T(8,128)(2,1)} %bitcast.50) | data formatting | bytes 33554432
  63.7 0.1 fusion.17
  63.8 0.1 fusion.19
  63.9 23.4 %fusion.5 = bf16[32,512,512]{2,1,0:T(8,128)(2,1)} fusion(bf16[512,512,1]{1,0,2:T(8,128)(2,1)S(1)} %bitcast.55, bf16[512,512,1]{1,0,2:T(8,128)(2,1)S(1)} %bitcast.54, bf16[1,32,512,512]{3,2,1,0:T(8,128)(2,1)} %param.9), kind=kOutput, calls=%fused_computation.7 | convolution fusion | flops 17196646400 | bytes 34603008 | tf_op jit(solution)/shard_map/npr,rs->nps/dot_general | solution.py:33
  87.2 18.5 %copy.55 = bf16[4,8,512,512]{3,1,2,0:T(8,128)(2,1)} copy(bf16[4,8,512,512]{3,2,1,0:T(8,128)(2,1)} %bitcast.51) | data formatting | bytes 33554432
  105.7 12.8 %convolution_bitcast_fusion = f32[32,32]{0,1:T(8,128)S(1)} fusion(bf16[32,262144]{1,0:T(8,128)(2,1)} %bitcast.49, bf16[32,262144]{1,0:T(8,128)(2,1)} %bitcast.48), kind=kOutput, calls=%fused_computation.9 | convolution fusion | flops 536870912 | bytes 33558528 | tf_op jit(solution)/shard_map/dot_general | solution.py:36
  118.5 0.1 copy.47
  118.6 0.2 reshape.74
  118.8 0.8 copy.52
  119.6 9.2 %all-to-all-start.2 = ((f32[128,2,2,2]{3,2,1,0:T(2,128)}), f32[128,2,2,2]{3,2,1,0:T(2,128)S(1)}, u32[]{:S(2)}, u32[]{:S(2)}) async-start(f32[128,2,2,2]{3,2,1,0:T(2,128)} %bitcast.10), calls=%async_computation.2 | async-start | bytes 524288 | tf_op jit(solution)/shard_map/all_to_all | solution.py:47
  128.8 0.2 all-reduce.3.cloned.1.call-start
  129.1 0.3 copy.44
  129.4 0.3 reshape.206
  129.7 2.1 copy.54
  131.8 8.4 %all-to-all-done.2 = f32[128,2,2,2]{3,2,1,0:T(2,128)S(1)} async-done(((f32[128,2,2,2]{3,2,1,0:T(2,128)}), f32[128,2,2,2]{3,2,1,0:T(2,128)S(1)}, u32[]{:S(2)}, u32[]{:S(2)}) %all-to-all-start.2) | async-done | bytes 4128 | tf_op jit(solution)/shard_map/all_to_all | solution.py:47
  140.3 0.3 reshape.208
  140.6 6.8 %scatter_fusion = f32[524288]{0:T(1024)S(1)} fusion(f32[524288]{0:T(1024)S(1)} %bitcast.47, s32[1024]{0:T(1024)S(1)} %reshape.206, f32[1024]{0:T(1024)S(1)} %reshape.208), kind=kCustom, calls=%fused_computation.1 | custom fusion | flops 1024 | bytes 16384
  147.4 1.5 reshape.81
  148.9 3.0 fusion.12
  152.0 115.2 %all-reduce.3.cloned.1.call-done = f32[1024,256]{1,0:T(8,128)} async-done(((f32[1024,256]{1,0:T(8,128)}), f32[1024,256]{1,0:T(8,128)}) %all-reduce.3.cloned.1.call-update) | async-done | bytes 1048592 | tf_op jit(solution)/shard_map/psum | solution.py:67
  267.2 1.9 dynamic-slice_select_fusion
  269.1 82.4 %all-reduce.5.cloned.1.call-done = f32[512,256]{1,0:T(8,128)} async-done(((f32[512,256]{1,0:T(8,128)}), f32[512,256]{1,0:T(8,128)}) %all-reduce.5.cloned.1.call-update) | async-done | bytes 524304 | tf_op jit(solution)/shard_map/psum | solution.py:12
  351.5 5.2 %convolution_subtract_fusion = f32[1024,512]{1,0:T(8,128)} fusion(f32[1024,512]{1,0:T(8,128)} %reshape.81, f32[1024,256]{1,0:T(8,128)} %all-reduce.3.cloned.1.call-done, f32[512,256]{1,0:T(8,128)} %all-reduce.5.cloned.1.call-done), kind=kOutput, calls=%fused_computation.8 | convolution fusion | flops 1611137024 | bytes 5767168 | tf_op jit(solution)/shard_map/dot_general | solution.py:70
  356.7 2.3 copy.60
  (22 shorter events, 0.2 us)
Async XLA Ops:
  7.2 8.8 %copy-start = (s32[8192]{0:T(1024)S(1)}, s32[8192]{0:T(1024)}, u32[]{:S(2)}) copy-start(s32[8192]{0:T(1024)} %param.11) | copy-start | bytes 98308
  7.2 31.9 %all-to-all-start = ((bf16[16,32,512]{2,1,0:T(8,128)(2,1)}), bf16[16,32,512]{2,1,0:T(8,128)(2,1)S(1)}, u32[]{:S(2)}, u32[]{:S(2)}) async-start(bf16[16,32,512]{2,1,0:T(8,128)(2,1)} %param.7), calls=%async_computation | async-start | bytes 1048576 | tf_op jit(solution)/shard_map/all_to_all | solution.py:22
  39.1 24.8 %all-to-all-start.1 = ((bf16[16,32,512]{2,1,0:T(8,128)(2,1)}), bf16[16,32,512]{2,1,0:T(8,128)(2,1)S(1)}, u32[]{:S(2)}, u32[]{:S(2)}) async-start(bf16[16,32,512]{2,1,0:T(8,128)(2,1)} %param.8), calls=%async_computation.1 | async-start | bytes 1048576 | tf_op jit(solution)/shard_map/all_to_all | solution.py:23
  45.1 18.5 %copy-start.3 = (s32[2]{0:T(128)S(1)}, s32[2]{0:T(128)}, u32[]{:S(2)}) copy-start(s32[2]{0:T(128)} %constant.102) | copy-start | bytes 28
  45.1 18.6 %copy-start.2 = (s32[2]{0:T(128)S(1)}, s32[2]{0:T(128)}, u32[]{:S(2)}) copy-start(s32[2]{0:T(128)} %constant.105) | copy-start | bytes 28
  119.6 20.6 %all-to-all-start.2 = ((f32[128,2,2,2]{3,2,1,0:T(2,128)}), f32[128,2,2,2]{3,2,1,0:T(2,128)S(1)}, u32[]{:S(2)}, u32[]{:S(2)}) async-start(f32[128,2,2,2]{3,2,1,0:T(2,128)} %bitcast.10), calls=%async_computation.2 | async-start | bytes 524288 | tf_op jit(solution)/shard_map/all_to_all | solution.py:47
  128.8 138.3 %all-reduce.3.cloned.1.call-start = ((), (), s32[]{:S(2)}) async-start(), calls=%async_computation.3 | async-start | bytes 2097152 | tf_op jit(solution)/shard_map/psum | solution.py:67
  140.6 218.4 %copy-start.1 = (s32[8192]{0:T(1024)S(1)}, s32[8192]{0:T(1024)}, u32[]{:S(2)}) copy-start(s32[8192]{0:T(1024)} %param.11) | copy-start | bytes 98308
  151.9 199.6 %all-reduce.5.cloned.1.call-start = ((), (), s32[]{:S(2)}) async-start(), calls=%async_computation.4 | async-start | bytes 1048576 | tf_op jit(solution)/shard_map/psum | solution.py:12
Sparse Core Ops, SparseCore 0:
  152.0 115.1 all-reduce.2
  270.4 81.0 all-reduce.4
where the time goes:
time: 371 us; the launch traced here: 366 us
  waiting for transfers between devices  206 us (56%)
  local copies, waits for them, and re-layouts  69.1 us (19%)
  matrix products  44.4 us (12%)
  starting transfers between devices  23 us (6%)
  between operations  14.2 us (4%)
  other arithmetic  8.92 us (2%)
    psum x1, waiting for transfers between devices, per_device(): panel_factor = lax.psum(partial_factor, 'col')  115 us
    psum x1, waiting for transfers between devices, broadcast(): return lax.psum(kept, axis)  82.4 us
    unnamed x15, local copies, waits for them, and re-layouts  42.8 us
    dot_general x1, matrix products, per_device(): jnp.einsum('npr,rs->nps', left_prod, inverse_dual, preferred_element_type...  23.4 us
    gather x2, local copies, waits for them, and re-layouts, per_device(): positions = jnp.take(con_pos, slot_con, axis=0)  23.1 us
    dot_general x1, matrix products, per_device(): lax.dot_general(constraint_slots.reshape(count, order * order), mapped_im...  12.8 us
    all_to_all x1, starting transfers between devices, per_device(): lax.all_to_all(outgoing, ('row', 'col'), split_axis=0, concat_axis=0, til...  9.19 us
    all_to_all x1, waiting for transfers between devices, per_device(): lax.all_to_all(outgoing, ('row', 'col'), split_axis=0, concat_axis=0, til...  8.43 us
  transfers between devices with their start and end apart: 5, of which 3 were waited for; matrix products, arithmetic and copies ran while one was open for 12% of the time, Pallas kernels for 0%

commit v1 on v0

v1 whole, which is shorter than its diff:
```python
import functools

import jax
import jax.numpy as jnp
from jax import lax
from jax.experimental import pallas as pl
from jax.experimental.pallas import tpu as pltpu
from jax.sharding import PartitionSpec as P

TILE = 16
PW = 256
PART = 512
MESH = pl.DeviceIdType.MESH
F32 = jnp.float32
BF16 = jnp.bfloat16
PRIMAL, DUAL, SLAB, PART_ROWS, ENTRIES, SLAB_ENTRIES, PART_ENTRIES = range(7)


def dot(a, b, dims=((1,), (0,)), precision=None):
    return lax.dot_general(a, b, (dims, ((), ())), precision=precision, preferred_element_type=F32)


def iota(shape, axis):
    return lax.broadcasted_iota(jnp.int32, shape, axis)


def halves(value):
    high = value.astype(BF16)
    return high, (value - high.astype(F32)).astype(BF16)


def dot_halves(a, b, dims=((1,), (0,))):
    a_high, a_low = a
    b_high, b_low = b
    return dot(a_high, b_high, dims) + dot(a_high, b_low, dims) + dot(a_low, b_high, dims)


def flag(condition):
    return jnp.where(condition, 1.0, 0.0).astype(BF16)


def assemble_kernel(
    n_row, n_col,
    moment_x, moment_s, coeffs, slot_con, con_pos, schur_prev,
    slab_panel, part_panel, slab_entries, part_entries, local_pos,
    a_v, left_v, x_v, s_v, wide_v, own_panel, total, entry_v, gathered, chosen,
    a_sem, own_sem, send_sem, recv_sem,
):
    row = lax.axis_index("row")
    col = lax.axis_index("col")
    count, order = a_v.shape[0], a_v.shape[1]
    chunk = order // n_col
    home = lax.div(col, n_col // n_row)

    a_parts = a_sem.shape[0]
    per_part = count // a_parts

    def a_copy(part):
        where = pl.ds(part * per_part, per_part)
        return pltpu.make_async_copy(coeffs.at[0, where], a_v.at[where], a_sem.at[part])

    my_chunk = pl.ds(pl.multiple_of(col * chunk, chunk), chunk)
    my_tile = pl.ds(pl.multiple_of(col * TILE, TILE), TILE)
    wide_copy = pltpu.make_async_copy(schur_prev.at[:, pl.ds(0, wide_v.shape[1])], wide_v, own_sem.at[4])
    own_x = pltpu.make_async_copy(moment_x.at[col], x_v.at[my_chunk], own_sem.at[PRIMAL])
    own_s = pltpu.make_async_copy(moment_s.at[col], s_v.at[my_chunk], own_sem.at[DUAL])
    wide_copy.start()
    own_x.start()
    own_s.start()
    lax.fori_loop(0, a_parts, lambda part, _: a_copy(part).start(), None)

    barrier = pltpu.get_barrier_semaphore()

    def greet(r, c):
        pl.semaphore_signal(barrier, inc=1, device_id=(r, c), device_id_type=MESH)

    lax.fori_loop(1, n_col, lambda k, _: greet(row, lax.rem(col + k, n_col)), None)
    lax.fori_loop(1, n_row, lambda k, _: greet(lax.rem(row + k, n_row), col), None)

    def greet_home(j, _):
        @pl.when(jnp.logical_or(home != row, j != col))
        def _():
            greet(home, j)

    lax.fori_loop(0, n_col, greet_home, None)
    at_home = home == row
    pl.semaphore_wait(barrier, n_col - 1 + n_row - 1 + n_col - at_home.astype(jnp.int32))

    def send(src, dst, which, r, c):
        pltpu.make_async_remote_copy(
            src_ref=src, dst_ref=dst, send_sem=send_sem.at[which], recv_sem=recv_sem.at[which],
            device_id=(r, c), device_id_type=MESH,
        ).start()

    def to_col(which, src, dst):
        def step(k, _):
            peer = lax.rem(col + k, n_col)
            send(src(peer), dst, which, row, peer)
        lax.fori_loop(1, n_col, step, None)

    halves_here = n_col // n_row

    def to_parts(which, src, dst):
        def step(k, _):
            r = lax.rem(row + k, n_row)
            for half in range(halves_here):
                c = row * halves_here + half

                @pl.when(jnp.logical_or(r != row, c != col))
                def _():
                    send(src(half), dst, which, r, c)

                @pl.when(jnp.logical_and(r == row, c == col))
                def _():
                    pltpu.make_async_copy(src(half), dst, recv_sem.at[which]).start()
        lax.fori_loop(0, n_row, step, None)

    def wait_bytes(ref, sem):
        pltpu.make_async_copy(ref, ref, sem).wait()

    def wait_parts_sent(which, whole, less):
        @pl.when(at_home)
        def _():
            wait_bytes(less, send_sem.at[which])

        @pl.when(jnp.logical_not(at_home))
        def _():
            wait_bytes(whole, send_sem.at[which])

    to_col(PRIMAL, lambda peer: moment_x.at[peer], x_v.at[my_chunk])
    to_col(DUAL, lambda peer: moment_s.at[peer], s_v.at[my_chunk])

    blocks = slot_con.shape[0]
    con = slot_con[...]
    perm = flag(iota((blocks, blocks), 1) == (iota((blocks, blocks), 0) % n_col) * n_row + iota((blocks, blocks), 0) // n_col)
    lanes = con_pos.shape[1]
    con_high = dot((con // lanes).astype(F32).astype(BF16), perm, ((0,), (0,)))
    con_low = dot((con % lanes).astype(F32).astype(BF16), perm, ((0,), (0,)))
    table = ((con_pos[...] % PART) - PART // 2).astype(F32).astype(BF16)
    high_iota = iota((con_pos.shape[0], blocks), 0).astype(F32)
    low_iota = iota((lanes, blocks), 0).astype(F32)
    for t in range(count):
        picked = dot(table, flag(high_iota == con_high[t:t + 1, :]), ((0,), (0,)))
        local_pos[t:t + 1, :] = jnp.sum(jnp.where(low_iota == con_low[t:t + 1, :], picked, 0.0), axis=0, keepdims=True)

    wide_copy.wait()
    own_panel[...] = jnp.transpose(wide_v[...])[:TILE, :]

    own_x.wait()
    wait_bytes(x_v.at[pl.ds(0, order - chunk)], recv_sem.at[PRIMAL])
    own_slab = pltpu.make_async_copy(own_panel, slab_panel.at[my_tile], own_sem.at[SLAB])
    own_slab.start()
    to_col(SLAB, lambda peer: own_panel, slab_panel.at[my_tile])
    to_parts(PART_ROWS, lambda half: own_panel.at[:, pl.ds(half * PART, PART)], part_panel.at[my_tile])

    def lefts(part, _):
        a_copy(part).wait()
        for i in range(per_part):
            t = part * per_part + i
            left_v[t] = dot(x_v[...], a_v[t]).astype(BF16)

    lax.fori_loop(0, a_parts, lefts, None)

    own_s.wait()
    wait_bytes(s_v.at[pl.ds(0, order - chunk)], recv_sem.at[DUAL])
    total[...] = jnp.zeros_like(total)
    side = total.shape[0]

    def images(g, _):
        rows = pl.ds(pl.multiple_of(g * 16, 16), 16)
        image = dot(left_v[:, rows, :].reshape(count * 16, order), s_v[...]).reshape(count, 2, 8, order)
        coeff = a_v[:, rows, :].astype(F32).reshape(count, 2, 8, order)
        for h in range(2):
            total[...] += dot(
                coeff[:, h].reshape(side, order).astype(BF16), image[:, h].reshape(side, order).astype(BF16), ((1,), (1,))
            )

    lax.fori_loop(0, order // 16, images, None)

    per_row = count // n_row
    kept = jnp.where(iota((side, side), 0) % 8 == iota((side, side), 1) % 8, total[...], 0.0)
    by_slot = jnp.sum(kept.reshape(count, 8, side), axis=1)
    fold = jnp.where(iota((side, per_row * count), 1) % count == iota((side, per_row * count), 0) // 8, 1.0, 0.0)
    spread = dot(by_slot, fold, precision=lax.Precision.HIGHEST)
    spread = jnp.where(iota(spread.shape, 1) // count == iota(spread.shape, 0) % per_row, spread, 0.0)
    pack = jnp.where(iota((n_row, count), 1) // per_row == iota((n_row, count), 0), 1.0, 0.0)
    packed = dot(pack, spread, precision=lax.Precision.HIGHEST)
    entry_v[...] = packed
    gathered[pl.ds(row, 1)] = packed[None]

    def to_row(k, _):
        peer = lax.rem(row + k, n_row)
        send(entry_v, gathered.at[row], ENTRIES, peer, col)

    lax.fori_loop(1, n_row, to_row, None)
    wait_bytes(gathered.at[pl.ds(0, n_row - 1)], recv_sem.at[ENTRIES])
    every = gathered[...]
    chosen[...] = jnp.sum(jnp.where(iota(every.shape, 1) == row, every, 0.0), axis=1)
    own_entries = pltpu.make_async_copy(chosen, slab_entries.at[col], own_sem.at[3])
    own_entries.start()
    to_col(SLAB_ENTRIES, lambda peer: chosen, slab_entries.at[col])
    to_parts(PART_ENTRIES, lambda half: chosen, part_entries.at[col])

    own_slab.wait()
    wait_bytes(slab_panel.at[pl.ds(0, PW - TILE)], recv_sem.at[SLAB])
    wait_bytes(part_panel, recv_sem.at[PART_ROWS])
    wait_bytes(x_v.at[pl.ds(0, order - chunk)], send_sem.at[PRIMAL])
    wait_bytes(s_v.at[pl.ds(0, order - chunk)], send_sem.at[DUAL])
    wait_bytes(slab_panel.at[pl.ds(0, PW - TILE)], send_sem.at[SLAB])
    wait_parts_sent(PART_ROWS, part_panel, part_panel.at[pl.ds(0, PW - TILE)])
    wait_bytes(gathered.at[pl.ds(0, n_row - 1)], send_sem.at[ENTRIES])
    own_entries.wait()
    wait_bytes(slab_entries.at[pl.ds(0, n_col - 1)], recv_sem.at[SLAB_ENTRIES])
    wait_bytes(part_entries, recv_sem.at[PART_ENTRIES])
    wait_bytes(slab_entries.at[pl.ds(0, n_col - 1)], send_sem.at[SLAB_ENTRIES])
    wait_parts_sent(PART_ENTRIES, part_entries, part_entries.at[pl.ds(0, n_col - 1)])


def finish_kernel(
    n_row, n_col,
    schur_prev, slab_panel, part_panel, slab_entries, part_entries, local_pos, panel_inv,
    updated, panel_factor,
    added, inv_high, inv_low, other_high, other_low,
):
    step = pl.program_id(0)
    row = lax.axis_index("row")
    col = lax.axis_index("col")
    slots, blocks = local_pos.shape
    per_row = slots // n_row
    pos = local_pos[...]

    def slot_lanes(slot):
        return jnp.sum(jnp.where(iota(pos.shape, 0) == slot, pos, 0.0), axis=0, keepdims=True) + PART // 2

    @pl.when(step == 0)
    def _():
        pos16 = pos.astype(BF16)
        high, low = halves(panel_inv[...])
        inv_high[...] = high
        inv_low[...] = low
        key = iota((2 * blocks, PW), 0) % blocks
        tile = iota((2 * blocks, PW), 1) // TILE
        in_tile = []
        for u in range(2):
            pick = flag(iota((slots, PW), 0) == 2 * (iota((slots, PW), 1) // TILE) + u)
            local = dot(pos16, pick, ((0,), (0,)))
            in_tile.append(local == (iota((blocks, PW), 1) % TILE - PART // 2).astype(F32))

        def panel_terms(entries, s4):
            terms = [
                jnp.where(in_tile[u], dot(entries, flag(key == s4 * slots + 2 * tile + u)), 0.0) for u in range(2)
            ]
            return terms[0] + terms[1]

        own = jnp.concatenate(halves(slab_entries[...].reshape(blocks, -1)), axis=1)
        own_key = iota((2 * blocks, PART), 0) % blocks
        in_part = []
        for u in range(2):
            local = dot(pos16, flag(iota((slots, PART), 0) == 2 * col + u), ((0,), (0,)))
            in_part.append(local == (iota((blocks, PART), 1) - PART // 2).astype(F32))
        for s4 in range(per_row):
            here = pl.ds(s4 * blocks, blocks)
            there = pl.ds((per_row + s4) * blocks, blocks)
            high, low = halves(panel_terms(own, s4))
            added[here, 0:PW] = high
            added[there, 0:PW] = low
            terms = [
                jnp.where(in_part[u], dot(own, flag(own_key == s4 * slots + 2 * col + u)), 0.0) for u in range(2)
            ]
            high, low = halves(terms[0] + terms[1])
            added[here, PW:] = high
            added[there, PW:] = low

        other = jnp.concatenate(halves(part_entries[...].reshape(blocks, -1)), axis=1)
        panel = jnp.transpose(part_panel[...])
        for u in range(2):
            high, low = halves(panel_terms(other, 2 * lax.rem(col, n_col // n_row) + u))
            at = flag(iota((PART, blocks), 0).astype(F32) == slot_lanes(2 * col + u))
            panel += dot(at, high) + dot(at, low)
        high, low = halves(dot_halves(halves(panel), (inv_high[...], inv_low[...])))
        other_high[...] = high
        other_low[...] = low

    tall = updated.shape[0]
    at = []
    for s4 in range(per_row):
        place = slot_lanes(per_row * row + s4) + (s4 // 2) * PART
        at.append(flag((iota((tall, blocks), 0) + step * tall).astype(F32) == place))
    at = jnp.concatenate(at + at, axis=1)
    sums = dot(at, added[...])
    panel = jnp.transpose(slab_panel[...]) + sums[:, :PW]
    factor = dot_halves(halves(panel), (inv_high[...], inv_low[...]))
    panel_factor[...] = factor
    updated[...] = (
        schur_prev[...] + sums[:, PW:] - dot_halves(halves(factor), (other_high[...], other_low[...]), ((1,), (1,)))
    )


def per_device(n_row, n_col, moment_x, moment_s, coeffs, slot_con, con_pos, schur_prev, panel_inv):
    count, order = coeffs.shape[1], coeffs.shape[2]
    blocks = slot_con.shape[0]
    slab, part = schur_prev.shape
    vmem = pl.BlockSpec(memory_space=pltpu.VMEM)
    hbm = pl.BlockSpec(memory_space=pl.ANY)
    tile = (n_row, (count // n_row) * count)
    side = count * 8
    slab_panel, part_panel, slab_entries, part_entries, local_pos = pl.pallas_call(
        functools.partial(assemble_kernel, n_row, n_col),
        out_shape=(
            jax.ShapeDtypeStruct((PW, slab), F32),
            jax.ShapeDtypeStruct((PW, part), F32),
            jax.ShapeDtypeStruct((n_col,) + tile, F32),
            jax.ShapeDtypeStruct((n_col,) + tile, F32),
            jax.ShapeDtypeStruct((count, blocks), F32),
        ),
        in_specs=[hbm, hbm, hbm, vmem, vmem, hbm],
        out_specs=(hbm, hbm, hbm, hbm, vmem),
        scratch_shapes=[
            pltpu.VMEM((count, order, order), BF16),
            pltpu.VMEM((count, order, order), BF16),
            pltpu.VMEM((order, order), BF16),
            pltpu.VMEM((order, order), BF16),
            pltpu.VMEM((slab, 128), F32),
            pltpu.VMEM((TILE, slab), F32),
            pltpu.VMEM((side, side), F32),
            pltpu.VMEM(tile, F32),
            pltpu.VMEM((n_row,) + tile, F32),
            pltpu.VMEM(tile, F32),
            pltpu.SemaphoreType.DMA((8,)),
            pltpu.SemaphoreType.DMA((5,)),
            pltpu.SemaphoreType.DMA((7,)),
            pltpu.SemaphoreType.DMA((7,)),
        ],
        compiler_params=pltpu.CompilerParams(
            collective_id=0, has_side_effects=True, vmem_limit_bytes=56 * 2**20
        ),
    )(moment_x, moment_s, coeffs, slot_con, con_pos.reshape(-1, 128), schur_prev)

    steps = 4
    tall = slab // steps
    whole = lambda *shape: pl.BlockSpec(shape, lambda i: (0,) * len(shape))
    return pl.pallas_call(
        functools.partial(finish_kernel, n_row, n_col),
        grid=(steps,),
        out_shape=(jax.ShapeDtypeStruct((slab, part), F32), jax.ShapeDtypeStruct((slab, PW), F32)),
        in_specs=[
            pl.BlockSpec((tall, part), lambda i: (i, 0)),
            pl.BlockSpec((PW, tall), lambda i: (0, i)),
            whole(PW, part),
            whole(n_col, *tile),
            whole(n_col, *tile),
            whole(count, blocks),
            whole(PW, PW),
        ],
        out_specs=(pl.BlockSpec((tall, part), lambda i: (i, 0)), pl.BlockSpec((tall, PW), lambda i: (i, 0))),
        scratch_shapes=[
            pltpu.VMEM((2 * blocks * (count // n_row), PW + part), BF16),
            pltpu.VMEM((PW, PW), BF16),
            pltpu.VMEM((PW, PW), BF16),
            pltpu.VMEM((part, PW), BF16),
            pltpu.VMEM((part, PW), BF16),
        ],
        compiler_params=pltpu.CompilerParams(vmem_limit_bytes=48 * 2**20),
    )(schur_prev, slab_panel, part_panel, slab_entries, part_entries, local_pos, panel_inv)


def solution(mesh):
    placed = (
        P("row", "col", None),
        P("row", "col", None),
        P(("row", "col"), None, None, None),
        P(),
        P(),
        P("row", "col"),
        P(),
    )
    return jax.shard_map(
        functools.partial(per_device, mesh.shape["row"], mesh.shape["col"]),
        mesh=mesh,
        in_specs=placed,
        out_specs=(P("row", "col"), P("row", None)),
        check_vma=False,
    )
```

time: 371 us -> 89.6 us (0.24); the launches traced: 366 us -> 89.2 us
  waiting for transfers between devices: 206 us -> 0 us
  Pallas kernels: 0 us -> 82.4 us
  local copies, waits for them, and re-layouts: 69.1 us -> 6.11 us
  matrix products: 44.4 us -> 0 us
  starting transfers between devices: 23 us -> 0 us
  between operations: 14.2 us -> 0.67 us
  other arithmetic: 8.92 us -> 0 us
    psum x2 -> x0, waiting for transfers between devices: 198 us -> none  [the longest x1 115 us: per_device(): panel_factor = lax.psum(partial_factor, 'col')]
    pallas_call x0 -> x2, Pallas kernels: none -> 82.4 us  [the longest x1 75.5 us: per_device(): pl.pallas_call(functools.partial(assemble_kernel, n_row, n_col), out_shap...]
    dot_general x4 -> x0, matrix products: 44.4 us -> none  [the longest x1 23.4 us: per_device(): jnp.einsum('npr,rs->nps', left_prod, inverse_dual, preferred_element_type...]
    unnamed x15, local copies, waits for them, and re-layouts: 42.8 us -> 6.11 us
    gather x2 -> x0, local copies, waits for them, and re-layouts: 23.1 us -> none  [per_device(): positions = jnp.take(con_pos, slot_con, axis=0)]
    all_to_all x3 -> x0, starting transfers between devices: 22.8 us -> none  [the longest x1 9.19 us: per_device(): lax.all_to_all(outgoing, ('row', 'col'), split_axis=0, concat_axis=0, til...]
    all_to_all x3 -> x0, waiting for transfers between devices: 8.43 us -> none  [the longest x1 8.43 us: per_device(): lax.all_to_all(outgoing, ('row', 'col'), split_axis=0, concat_axis=0, til...]
    unnamed x4 -> x0, other arithmetic: 7 us -> none
  transfers between devices with their start and end apart: 5 -> 0, of which waited for: 3 -> 0; matrix products, arithmetic and copies ran while one was open for 12% -> 0% of each run, Pallas kernels for 0% -> 0%
where the time goes in v1:
time: 89.6 us; the launch traced here: 89.2 us
  Pallas kernels  82.4 us (92%)
  local copies, waits for them, and re-layouts  6.11 us (7%)
    pallas_call x1, Pallas kernels, per_device(): pl.pallas_call(functools.partial(assemble_kernel, n_row, n_col), out_shap...  75.5 us
    pallas_call x1, Pallas kernels, per_device(): pl.pallas_call(functools.partial(finish_kernel, n_row, n_col), grid=(step...  6.9 us
    unnamed x15, local copies, waits for them, and re-layouts  6.11 us

profile of v1, /device:TPU:1, one launch (start us, length us, event | category | flops | bytes accessed | tf_op | source)
XLA Modules:
  0.0 89.2 jit_solution(11866737178829145091)
XLA Ops:
  0.6 1.4 %copy.9.slot_con = s32[128,32]{1,0:T(8,128)} copy(s32[128,32]{0,1:T(8,128)} %param.10) | data formatting | bytes 32768 | tf_op args[3]
  2.1 0.0 copy-start
  2.1 0.0 copy-start.3
  2.1 75.5 %shard_map.86 = (f32[256,1024]{1,0:T(8,128)}, f32[256,512]{1,0:T(8,128)}, f32[16,8,128]{2,1,0:T(8,128)}, f32[16,8,128]{2,1,0:T(8,128)}, f32[32,128]{1,0:T(8,128)}) custom-call(bf16[16,32,512]{2,1,0:T(8,128)(2,1)} %moment_x.1, bf16[16,32,512]{2,1,0:T(8,128)(2,1)} %moment_s.1, bf16[1,32,512,512]{3,2,1,0:T(8,128)(2,1)} %coeffs.1, s32[128,32]{1,0:T(8,128)} %copy.9.slot_con, ...), custom_call_target="tpu_custom_call" | custom-call | tf_op jit(solution)/shard_map/pallas_call | solution.py:307
  77.6 0.0 copy-done
  77.6 0.0 copy-done.3
  77.6 0.0 copy-start.1
  77.6 1.2 %copy-done.1 = f32[256,1024]{1,0:T(8,128)S(1)} copy-done((f32[256,1024]{1,0:T(8,128)S(1)}, f32[256,1024]{1,0:T(8,128)}, u32[]{:S(2)}) %copy-start.1) | copy-done | bytes 1048600
  78.9 0.0 copy-start.2
  78.9 1.0 %copy-done.2 = f32[256,512]{1,0:T(8,128)S(1)} copy-done((f32[256,512]{1,0:T(8,128)S(1)}, f32[256,512]{1,0:T(8,128)}, u32[]{:S(2)}) %copy-start.2) | copy-done | bytes 524312
  79.9 0.0 copy-start.4
  79.9 0.8 copy-done.4
  80.7 0.0 copy-start.5
  80.7 0.8 copy-done.5
  81.6 0.0 copy-start.6
  81.6 0.7 copy-done.6
  82.3 6.9 %shard_map.87 = (f32[1024,512]{1,0:T(8,128)}, f32[1024,256]{1,0:T(8,128)}) custom-call(f32[1024,512]{1,0:T(8,128)S(1)} %copy-done, f32[256,1024]{1,0:T(8,128)S(1)} %copy-done.1, f32[256,512]{1,0:T(8,128)S(1)} %copy-done.2, f32[16,8,128]{2,1,0:T(8,128)S(1)} %copy-done.4, f32[16,8,128]{2,1,0:T(8,128)S(1)} %copy-done.5, f32[32,128]{1,0:T(8,128)S(1)} %copy-done.6, ...), custom_call_target="tpu_custom_call" | custom-call | tf_op jit(solution)/shard_map/pallas_call | solution.py:342
Async XLA Ops:
  2.1 75.5 %copy-start = (f32[1024,512]{1,0:T(8,128)S(1)}, f32[1024,512]{1,0:T(8,128)}, u32[]{:S(2)}) copy-start(f32[1024,512]{1,0:T(8,128)} %schur_prev.3) | copy-start | bytes 6291460
  2.1 75.5 %copy-start.3 = (f32[256,256]{1,0:T(8,128)S(1)}, f32[256,256]{1,0:T(8,128)}, u32[]{:S(2)}) copy-start(f32[256,256]{1,0:T(8,128)} %panel_inv.1) | copy-start | bytes 786436
  77.6 1.2 %copy-start.1 = (f32[256,1024]{1,0:T(8,128)S(1)}, f32[256,1024]{1,0:T(8,128)}, u32[]{:S(2)}) copy-start(f32[256,1024]{1,0:T(8,128)} %get-tuple-element.7.slab_panel) | copy-start | bytes 3145732
  78.9 1.0 %copy-start.2 = (f32[256,512]{1,0:T(8,128)S(1)}, f32[256,512]{1,0:T(8,128)}, u32[]{:S(2)}) copy-start(f32[256,512]{1,0:T(8,128)} %get-tuple-element.8.part_panel) | copy-start | bytes 1572868
  79.9 0.8 copy-start.4
  80.7 0.8 copy-start.5
  81.6 0.7 copy-start.6

commit v2 on v1

v2 whole, which is shorter than its diff:
```python
import functools

import jax
import jax.numpy as jnp
from jax import lax
from jax.experimental import pallas as pl
from jax.experimental.pallas import tpu as pltpu
from jax.sharding import PartitionSpec as P

TILE = 16
PW = 256
PART = 512
MESH = pl.DeviceIdType.MESH
F32 = jnp.float32
BF16 = jnp.bfloat16
PRIMAL, DUAL, SLAB, SLAB_PASSED, PART_ROWS, ENTRIES, PAIRS = range(7)


def dot(a, b, dims=((1,), (0,)), precision=None):
    return lax.dot_general(a, b, (dims, ((), ())), precision=precision, preferred_element_type=F32)


def iota(shape, axis):
    return lax.broadcasted_iota(jnp.int32, shape, axis)


def halves(value):
    high = value.astype(BF16)
    return high, (value - high.astype(F32)).astype(BF16)


def dot_halves(a, b, dims=((1,), (0,))):
    a_high, a_low = a
    b_high, b_low = b
    return dot(a_high, b_high, dims) + dot(a_high, b_low, dims) + dot(a_low, b_high, dims)


def flag(condition):
    return jnp.where(condition, 1.0, 0.0).astype(BF16)


def assemble_kernel(
    n_row, n_col,
    moment_x, moment_s, coeffs, slot_con, con_pos, schur_prev,
    slab_panel, part_panel, entry_pairs, local_pos,
    a_v, left_v, x_v, s_v, wide_v, own_panel, total, image_v, entry_v, gathered, chosen,
    a_sem, own_sem, send_sem, recv_sem,
):
    row = lax.axis_index("row")
    col = lax.axis_index("col")
    count, order = a_v.shape[0], a_v.shape[1]
    chunk = order // n_col
    home = lax.div(col, n_col // n_row)

    a_parts = a_sem.shape[0]
    per_part = count // a_parts

    def a_copy(part):
        where = pl.ds(part * per_part, per_part)
        return pltpu.make_async_copy(coeffs.at[0, where], a_v.at[where], a_sem.at[part])

    my_chunk = pl.ds(pl.multiple_of(col * chunk, chunk), chunk)
    my_tile = pl.ds(pl.multiple_of(col * TILE, TILE), TILE)
    wide_copy = pltpu.make_async_copy(schur_prev.at[:, pl.ds(0, wide_v.shape[1])], wide_v, own_sem.at[4])
    own_x = pltpu.make_async_copy(moment_x.at[col], x_v.at[my_chunk], own_sem.at[PRIMAL])
    own_s = pltpu.make_async_copy(moment_s.at[col], s_v.at[my_chunk], own_sem.at[DUAL])
    wide_copy.start()
    own_x.start()
    own_s.start()
    lax.fori_loop(0, a_parts, lambda part, _: a_copy(part).start(), None)

    barrier = pltpu.get_barrier_semaphore()

    def greet(r, c):
        pl.semaphore_signal(barrier, inc=1, device_id=(r, c), device_id_type=MESH)

    lax.fori_loop(1, n_col, lambda k, _: greet(row, lax.rem(col + k, n_col)), None)
    lax.fori_loop(1, n_row, lambda k, _: greet(lax.rem(row + k, n_row), col), None)

    def greet_home(j, _):
        @pl.when(jnp.logical_or(home != row, j != col))
        def _():
            greet(home, j)

    lax.fori_loop(0, n_col, greet_home, None)
    at_home = home == row
    pl.semaphore_wait(barrier, n_col - 1 + n_row - 1 + n_col - at_home.astype(jnp.int32))

    def send(src, dst, which, r, c):
        pltpu.make_async_remote_copy(
            src_ref=src, dst_ref=dst, send_sem=send_sem.at[which], recv_sem=recv_sem.at[which],
            device_id=(r, c), device_id_type=MESH,
        ).start()

    def to_col(which, src, dst):
        def step(k, _):
            peer = lax.rem(col + k, n_col)
            send(src(peer), dst, which, row, peer)
        lax.fori_loop(1, n_col, step, None)

    halves_here = n_col // n_row

    def to_parts(which, src, dst):
        def step(k, _):
            r = lax.rem(row + k, n_row)
            for half in range(halves_here):
                c = row * halves_here + half

                @pl.when(jnp.logical_or(r != row, c != col))
                def _():
                    send(src(half), dst, which, r, c)

                @pl.when(jnp.logical_and(r == row, c == col))
                def _():
                    pltpu.make_async_copy(src(half), dst, recv_sem.at[which]).start()
        lax.fori_loop(0, n_row, step, None)

    def wait_bytes(ref, sem):
        pltpu.make_async_copy(ref, ref, sem).wait()

    def wait_parts_sent(which, whole, less):
        @pl.when(at_home)
        def _():
            wait_bytes(less, send_sem.at[which])

        @pl.when(jnp.logical_not(at_home))
        def _():
            wait_bytes(whole, send_sem.at[which])

    to_col(PRIMAL, lambda peer: moment_x.at[peer], x_v.at[my_chunk])
    to_col(DUAL, lambda peer: moment_s.at[peer], s_v.at[my_chunk])

    blocks = slot_con.shape[1]
    con = slot_con[...]
    perm = flag(iota((blocks, blocks), 1) == (iota((blocks, blocks), 0) % n_col) * n_row + iota((blocks, blocks), 0) // n_col)
    lanes = con_pos.shape[1]
    con_high = dot((con // lanes).astype(F32).astype(BF16), perm)
    con_low = dot((con % lanes).astype(F32).astype(BF16), perm)
    table = ((con_pos[...] % PART) - PART // 2).astype(F32).astype(BF16)
    high_iota = iota((con_pos.shape[0], blocks), 0).astype(F32)
    low_iota = iota((lanes, blocks), 0).astype(F32)
    for t in range(count):
        picked = dot(table, flag(high_iota == con_high[t:t + 1, :]), ((0,), (0,)))
        local_pos[t:t + 1, :] = jnp.sum(jnp.where(low_iota == con_low[t:t + 1, :], picked, 0.0), axis=0, keepdims=True)

    wide_copy.wait()
    own_panel[...] = jnp.transpose(wide_v[...])[:TILE, :]

    own_x.wait()
    wait_bytes(x_v.at[pl.ds(0, order - chunk)], recv_sem.at[PRIMAL])
    sibling = lax.bitwise_xor(col, 1)
    others = n_col // 2 - 1
    own_slab = pltpu.make_async_copy(own_panel, slab_panel.at[my_tile], own_sem.at[SLAB])
    own_slab.start()
    send(own_panel, slab_panel.at[my_tile], SLAB_PASSED, row, sibling)

    def to_chip(k, _):
        send(own_panel, slab_panel.at[my_tile], SLAB, row, lax.rem(col + 2 * k, n_col))

    lax.fori_loop(1, n_col // 2, to_chip, None)
    to_parts(PART_ROWS, lambda half: own_panel.at[:, pl.ds(half * PART, PART)], part_panel.at[my_tile])

    def lefts(part, _):
        a_copy(part).wait()
        for i in range(per_part):
            t = part * per_part + i
            left_v[:, t] = dot(x_v[...], a_v[t]).astype(BF16).reshape(groups, 16, order)

    groups = order // 16
    lax.fori_loop(0, a_parts, lefts, None)

    own_s.wait()
    wait_bytes(s_v.at[pl.ds(0, order - chunk)], recv_sem.at[DUAL])
    side = total.shape[0]
    total[...] = jnp.zeros_like(total)
    image_v[1] = jnp.zeros_like(image_v[1])

    def by_eights(value):
        value = value.reshape(count, 2, 8, order)
        return jnp.concatenate([value[:, h].reshape(side, order).astype(BF16) for h in range(2)], axis=1)

    def add_entries(g, slot):
        rows = pl.ds(pl.multiple_of(g * 16, 16), 16)
        total[...] += dot(by_eights(a_v[:, rows, :].astype(F32)), image_v[slot], ((1,), (1,)))

    unroll = 4

    def images(q, _):
        for i in range(unroll):
            g = q * unroll + i
            image = dot(left_v[g].reshape(count * 16, order), s_v[...])
            add_entries(jnp.maximum(g - 1, 0) if i == 0 else g - 1, (i + 1) % 2)
            image_v[i % 2] = by_eights(image)

    lax.fori_loop(0, groups // unroll // 2, images, None)

    wait_bytes(slab_panel.at[pl.ds(0, others * TILE)], recv_sem.at[SLAB])

    def pass_on(k, _):
        peer = lax.rem(col + 2 * k, n_col)
        tile = slab_panel.at[pl.ds(pl.multiple_of(peer * TILE, TILE), TILE)]
        send(tile, tile, SLAB_PASSED, row, sibling)

    lax.fori_loop(1, n_col // 2, pass_on, None)

    lax.fori_loop(groups // unroll // 2, groups // unroll, images, None)
    add_entries(groups - 1, 1)

    per_row = count // n_row
    kept = jnp.where(iota((side, side), 0) % 8 == iota((side, side), 1) % 8, total[...], 0.0)
    by_slot = jnp.sum(kept.reshape(count, 8, side), axis=1)
    fold = jnp.where(iota((side, per_row * count), 1) % count == iota((side, per_row * count), 0) // 8, 1.0, 0.0)
    spread = dot(by_slot, fold, precision=lax.Precision.HIGHEST)
    spread = jnp.where(iota(spread.shape, 1) // count == iota(spread.shape, 0) % per_row, spread, 0.0)
    pack = jnp.where(iota((n_row, count), 1) // per_row == iota((n_row, count), 0), 1.0, 0.0)
    packed = dot(pack, spread, precision=lax.Precision.HIGHEST)
    entry_v[...] = packed
    gathered[pl.ds(row, 1)] = packed[None]

    def to_row(k, _):
        peer = lax.rem(row + k, n_row)
        send(entry_v, gathered.at[row], ENTRIES, peer, col)

    lax.fori_loop(1, n_row, to_row, None)
    wait_bytes(gathered.at[pl.ds(0, n_row - 1)], recv_sem.at[ENTRIES])
    mine = jnp.sum(jnp.where(iota(gathered.shape, 1) == row, gathered[...], 0.0), axis=1)
    for q in range(n_row):
        chosen[q, 0] = mine
        chosen[q, 1] = gathered[:, q, :]
    own_entries = pltpu.make_async_copy(chosen.at[home], entry_pairs.at[col], own_sem.at[3])
    own_entries.start()
    to_col(PAIRS, lambda peer: chosen.at[lax.div(peer, n_col // n_row)], entry_pairs.at[col])

    own_slab.wait()
    wait_bytes(slab_panel.at[pl.ds(0, (others + 1) * TILE)], recv_sem.at[SLAB_PASSED])
    wait_bytes(part_panel, recv_sem.at[PART_ROWS])
    wait_bytes(x_v.at[pl.ds(0, order - chunk)], send_sem.at[PRIMAL])
    wait_bytes(s_v.at[pl.ds(0, order - chunk)], send_sem.at[DUAL])
    wait_bytes(slab_panel.at[pl.ds(0, others * TILE)], send_sem.at[SLAB])
    wait_bytes(slab_panel.at[pl.ds(0, (others + 1) * TILE)], send_sem.at[SLAB_PASSED])
    wait_parts_sent(PART_ROWS, part_panel, part_panel.at[pl.ds(0, PW - TILE)])
    wait_bytes(gathered.at[pl.ds(0, n_row - 1)], send_sem.at[ENTRIES])
    own_entries.wait()
    wait_bytes(entry_pairs.at[pl.ds(0, n_col - 1)], recv_sem.at[PAIRS])
    wait_bytes(entry_pairs.at[pl.ds(0, n_col - 1)], send_sem.at[PAIRS])


def finish_kernel(
    n_row, n_col,
    schur_prev, slab_panel, part_panel, entry_pairs, local_pos, panel_inv,
    updated, panel_factor,
    slab_v, part_v, pairs_v, pos_v, inv_v, updated_v, factor_v, added, in_sem, out_sem,
):
    loads = [
        pltpu.make_async_copy(src, dst, in_sem.at[k])
        for k, (src, dst) in enumerate(
            (
                (local_pos, pos_v), (entry_pairs, pairs_v), (part_panel, part_v), (panel_inv, inv_v),
                (slab_panel, slab_v), (schur_prev, updated_v),
            )
        )
    ]
    for load in loads:
        load.start()
    row = lax.axis_index("row")
    col = lax.axis_index("col")
    slots, blocks = local_pos.shape
    per_row = slots // n_row
    key = iota((2 * blocks, PW), 0) % blocks
    tile = iota((2 * blocks, PW), 1) // TILE
    own_key = iota((2 * blocks, PART), 0) % blocks
    loads[0].wait()
    pos = pos_v[...]
    pos16 = pos.astype(BF16)

    def slot_lanes(slot):
        return jnp.sum(jnp.where(iota(pos.shape, 0) == slot, pos, 0.0), axis=0, keepdims=True) + PART // 2

    in_tile, in_part = [], []
    for u in range(2):
        pick = flag(iota((slots, PW), 0) == 2 * (iota((slots, PW), 1) // TILE) + u)
        local = dot(pos16, pick, ((0,), (0,)))
        in_tile.append(local == (iota((blocks, PW), 1) % TILE - PART // 2).astype(F32))
        local = dot(pos16, flag(iota((slots, PART), 0) == 2 * col + u), ((0,), (0,)))
        in_part.append(local == (iota((blocks, PART), 1) - PART // 2).astype(F32))

    def panel_terms(entries, s4):
        terms = [jnp.where(in_tile[u], dot(entries, flag(key == s4 * slots + 2 * tile + u)), 0.0) for u in range(2)]
        return terms[0] + terms[1]

    loads[1].wait()
    own = jnp.concatenate(halves(pairs_v[:, 0].reshape(blocks, -1)), axis=1)
    for s4 in range(per_row):
        here = pl.ds(s4 * blocks, blocks)
        there = pl.ds((per_row + s4) * blocks, blocks)
        high, low = halves(panel_terms(own, s4))
        added[here, 0:PW] = high
        added[there, 0:PW] = low
        terms = [jnp.where(in_part[u], dot(own, flag(own_key == s4 * slots + 2 * col + u)), 0.0) for u in range(2)]
        high, low = halves(terms[0] + terms[1])
        added[here, PW:] = high
        added[there, PW:] = low

    other = jnp.concatenate(halves(pairs_v[:, 1].reshape(blocks, -1)), axis=1)
    loads[2].wait()
    panel = jnp.transpose(part_v[...])
    for u in range(2):
        high, low = halves(panel_terms(other, 2 * lax.rem(col, n_col // n_row) + u))
        at = flag(iota((PART, blocks), 0).astype(F32) == slot_lanes(2 * col + u))
        panel += dot(at, high) + dot(at, low)
    loads[3].wait()
    inverse = halves(inv_v[...])
    columns = halves(dot_halves(halves(panel), inverse))

    loads[4].wait()
    slab = schur_prev.shape[0]
    steps = out_sem.shape[1]
    tall = slab // steps
    writes = []
    for step in range(steps):
        rows = pl.ds(step * tall, tall)
        at = []
        for s4 in range(per_row):
            place = slot_lanes(per_row * row + s4) + (s4 // 2) * PART
            at.append(flag((iota((tall, blocks), 0) + step * tall).astype(F32) == place))
        sums = dot(jnp.concatenate(at + at, axis=1), added[...])
        panel = jnp.transpose(slab_v[:, rows]) + sums[:, :PW]
        factor = dot_halves(halves(panel), inverse)
        factor_v[rows] = factor
        writes.append(pltpu.make_async_copy(factor_v.at[rows], panel_factor.at[rows], out_sem.at[0, step]))
        writes[-1].start()
        if step == 0:
            loads[5].wait()
        updated_v[rows] = updated_v[rows] + sums[:, PW:] - dot_halves(halves(factor), columns, ((1,), (1,)))
        writes.append(pltpu.make_async_copy(updated_v.at[rows], updated.at[rows], out_sem.at[1, step]))
        writes[-1].start()
    for write in writes:
        write.wait()


def per_device(n_row, n_col, moment_x, moment_s, coeffs, slot_con, con_pos, schur_prev, panel_inv):
    count, order = coeffs.shape[1], coeffs.shape[2]
    blocks = slot_con.shape[0]
    slab, part = schur_prev.shape
    vmem = pl.BlockSpec(memory_space=pltpu.VMEM)
    hbm = pl.BlockSpec(memory_space=pltpu.HBM)
    tile = (n_row, (count // n_row) * count)
    side = count * 8
    slab_panel, part_panel, entry_pairs, local_pos = pl.pallas_call(
        functools.partial(assemble_kernel, n_row, n_col),
        out_shape=(
            jax.ShapeDtypeStruct((PW, slab), F32),
            jax.ShapeDtypeStruct((PW, part), F32),
            jax.ShapeDtypeStruct((n_col, 2) + tile, F32),
            jax.ShapeDtypeStruct((count, blocks), F32),
        ),
        in_specs=[hbm, hbm, hbm, vmem, vmem, hbm],
        out_specs=(hbm, hbm, hbm, vmem),
        scratch_shapes=[
            pltpu.VMEM((count, order, order), BF16),
            pltpu.VMEM((order // 16, count, 16, order), BF16),
            pltpu.VMEM((order, order), BF16),
            pltpu.VMEM((order, order), BF16),
            pltpu.VMEM((slab, 128), F32),
            pltpu.VMEM((TILE, slab), F32),
            pltpu.VMEM((side, side), F32),
            pltpu.VMEM((2, side, 2 * order), BF16),
            pltpu.VMEM(tile, F32),
            pltpu.VMEM((n_row,) + tile, F32),
            pltpu.VMEM((n_row, 2) + tile, F32),
            pltpu.SemaphoreType.DMA((4,)),
            pltpu.SemaphoreType.DMA((5,)),
            pltpu.SemaphoreType.DMA((7,)),
            pltpu.SemaphoreType.DMA((7,)),
        ],
        compiler_params=pltpu.CompilerParams(
            collective_id=0, has_side_effects=True, vmem_limit_bytes=54 * 2**20
        ),
    )(moment_x, moment_s, coeffs, slot_con.T, con_pos.reshape(-1, 128), schur_prev)

    steps = 4
    return pl.pallas_call(
        functools.partial(finish_kernel, n_row, n_col),
        out_shape=(jax.ShapeDtypeStruct((slab, part), F32), jax.ShapeDtypeStruct((slab, PW), F32)),
        in_specs=[hbm] * 6,
        out_specs=(hbm, hbm),
        scratch_shapes=[
            pltpu.VMEM((PW, slab), F32),
            pltpu.VMEM((PW, part), F32),
            pltpu.VMEM((n_col, 2) + tile, F32),
            pltpu.VMEM((count, blocks), F32),
            pltpu.VMEM((PW, PW), F32),
            pltpu.VMEM((slab, part), F32),
            pltpu.VMEM((slab, PW), F32),
            pltpu.VMEM((2 * blocks * (count // n_row), PW + part), BF16),
            pltpu.SemaphoreType.DMA((6,)),
            pltpu.SemaphoreType.DMA((2, steps)),
        ],
        compiler_params=pltpu.CompilerParams(vmem_limit_bytes=63 * 2**20),
    )(schur_prev, slab_panel, part_panel, entry_pairs, local_pos, panel_inv)


def solution(mesh):
    placed = (
        P("row", "col", None),
        P("row", "col", None),
        P(("row", "col"), None, None, None),
        P(),
        P(),
        P("row", "col"),
        P(),
    )
    return jax.shard_map(
        functools.partial(per_device, mesh.shape["row"], mesh.shape["col"]),
        mesh=mesh,
        in_specs=placed,
        out_specs=(P("row", "col"), P("row", None)),
        check_vma=False,
    )
```

time: 89.6 us -> 67.6 us (0.75)
  Pallas kernels: 82.4 us -> 66.7 us
  local copies, waits for them, and re-layouts: 6.11 us -> 0 us
    pallas_call x1, Pallas kernels: 75.5 us -> 59.1 us  [per_device(): pl.pallas_call(functools.partial(assemble_kernel, n_row, n_col), out_shap...]
    unnamed x15 -> x0, local copies, waits for them, and re-layouts: 6.11 us -> none
where the time goes in v2:
time: 67.6 us; the launch traced here: 67.3 us
  Pallas kernels  66.7 us (99%)
    pallas_call x1, Pallas kernels, per_device(): pl.pallas_call(functools.partial(assemble_kernel, n_row, n_col), out_shap...  59.1 us
    pallas_call x1, Pallas kernels, per_device(): pl.pallas_call(functools.partial(finish_kernel, n_row, n_col), out_shape=...  7.64 us

profile of v2, /device:TPU:1, one launch (start us, length us, event | category | flops | bytes accessed | tf_op | source)
XLA Modules:
  0.0 67.3 jit_solution(14802343987131996200)
XLA Ops:
  0.6 59.1 %shard_map.86 = (f32[256,1024]{1,0:T(8,128)}, f32[256,512]{1,0:T(8,128)}, f32[16,2,8,128]{3,2,1,0:T(8,128)}, f32[32,128]{1,0:T(8,128)}) custom-call(bf16[16,32,512]{2,1,0:T(8,128)(2,1)} %moment_x.1, bf16[16,32,512]{2,1,0:T(8,128)(2,1)} %moment_s.1, bf16[1,32,512,512]{3,2,1,0:T(8,128)(2,1)} %coeffs.1, s32[32,128]{1,0:T(8,128)} %bitcast.3, s32[64,128]{1,0:T(8,128)} %bitcast.2, ...), custom_call_target="tpu_custom_call" | custom-call | tf_op jit(solution)/shard_map/pallas_call | solution.py:349
  59.7 7.6 %shard_map.87 = (f32[1024,512]{1,0:T(8,128)}, f32[1024,256]{1,0:T(8,128)}) custom-call(f32[1024,512]{1,0:T(8,128)} %schur_prev.3, f32[256,1024]{1,0:T(8,128)} %get-tuple-element.6.slab_panel, f32[256,512]{1,0:T(8,128)} %get-tuple-element.7.part_panel, f32[16,2,8,128]{3,2,1,0:T(8,128)} %get-tuple-element.8.entry_pairs, f32[32,128]{1,0:T(8,128)} %get-tuple-element.9.local_pos, ...), custom_call_target="tpu_custom_call" | custom-call | tf_op jit(solution)/shard_map/pallas_call | solution.py:382

commit v3 on v2

--- a/solution.py
+++ b/solution.py
@@ -13,7 +13,7 @@
 MESH = pl.DeviceIdType.MESH
 F32 = jnp.float32
 BF16 = jnp.bfloat16
-PRIMAL, DUAL, SLAB, SLAB_PASSED, PART_ROWS, ENTRIES, PAIRS = range(7)
+PRIMAL, DUAL, SLAB, SLAB_PASSED, PART_ROWS, PAIRS = range(6)
 
 
 def dot(a, b, dims=((1,), (0,)), precision=None):
@@ -43,8 +43,8 @@
     n_row, n_col,
     moment_x, moment_s, coeffs, slot_con, con_pos, schur_prev,
     slab_panel, part_panel, entry_pairs, local_pos,
-    a_v, left_v, x_v, s_v, wide_v, own_panel, total, image_v, entry_v, gathered, chosen,
-    a_sem, own_sem, send_sem, recv_sem,
+    a_v, left_v, x_v, s_v, wide_v, own_panel, total, image_v, chosen,
+    a_sem, own_sem, send_sem, recv_sem, everyone,
 ):
     row = lax.axis_index("row")
     col = lax.axis_index("col")
@@ -77,14 +77,11 @@
     lax.fori_loop(1, n_col, lambda k, _: greet(row, lax.rem(col + k, n_col)), None)
     lax.fori_loop(1, n_row, lambda k, _: greet(lax.rem(row + k, n_row), col), None)
 
-    def greet_home(j, _):
-        @pl.when(jnp.logical_or(home != row, j != col))
-        def _():
-            greet(home, j)
-
-    lax.fori_loop(0, n_col, greet_home, None)
     at_home = home == row
-    pl.semaphore_wait(barrier, n_col - 1 + n_row - 1 + n_col - at_home.astype(jnp.int32))
+    pl.semaphore_wait(barrier, n_col - 1 + n_row - 1)
+
+    def all_here(k, _):
+        pl.semaphore_signal(everyone, inc=1, device_id=(lax.rem(row + k, n_row), col), device_id_type=MESH)
 
     def send(src, dst, which, r, c):
         pltpu.make_async_remote_copy(
@@ -128,7 +125,7 @@
             wait_bytes(whole, send_sem.at[which])
 
     to_col(PRIMAL, lambda peer: moment_x.at[peer], x_v.at[my_chunk])
-    to_col(DUAL, lambda peer: moment_s.at[peer], s_v.at[my_chunk])
+    lax.fori_loop(1, n_row, all_here, None)
 
     blocks = slot_con.shape[1]
     con = slot_con[...]
@@ -143,11 +140,27 @@
         picked = dot(table, flag(high_iota == con_high[t:t + 1, :]), ((0,), (0,)))
         local_pos[t:t + 1, :] = jnp.sum(jnp.where(low_iota == con_low[t:t + 1, :], picked, 0.0), axis=0, keepdims=True)
 
+    wait_bytes(x_v.at[pl.ds(0, order - chunk)], send_sem.at[PRIMAL])
+    to_col(DUAL, lambda peer: moment_s.at[peer], s_v.at[my_chunk])
+
     wide_copy.wait()
     own_panel[...] = jnp.transpose(wide_v[...])[:TILE, :]
 
     own_x.wait()
     wait_bytes(x_v.at[pl.ds(0, order - chunk)], recv_sem.at[PRIMAL])
+    def lefts(part, _):
+        a_copy(part).wait()
+        for i in range(per_part):
+            t = part * per_part + i
+            left_v[:, t] = dot(x_v[...], a_v[t]).astype(BF16).reshape(groups, 16, order)
+
+    groups = order // 16
+    lax.fori_loop(0, a_parts, lefts, None)
+
+    own_s.wait()
+    wait_bytes(s_v.at[pl.ds(0, order - chunk)], recv_sem.at[DUAL])
+    pl.semaphore_wait(everyone, n_row - 1)
+
     sibling = lax.bitwise_xor(col, 1)
     others = n_col // 2 - 1
     own_slab = pltpu.make_async_copy(own_panel, slab_panel.at[my_tile], own_sem.at[SLAB])
@@ -160,18 +173,8 @@
     lax.fori_loop(1, n_col // 2, to_chip, None)
     to_parts(PART_ROWS, lambda half: own_panel.at[:, pl.ds(half * PART, PART)], part_panel.at[my_tile])
 
-    def lefts(part, _):
-        a_copy(part).wait()
-        for i in range(per_part):
-            t = part * per_part + i
-            left_v[:, t] = dot(x_v[...], a_v[t]).astype(BF16).reshape(groups, 16, order)
-
-    groups = order // 16
-    lax.fori_loop(0, a_parts, lefts, None)
-
-    own_s.wait()
-    wait_bytes(s_v.at[pl.ds(0, order - chunk)], recv_sem.at[DUAL])
     side = total.shape[0]
+    per_row = count // n_row
     total[...] = jnp.zeros_like(total)
     image_v[1] = jnp.zeros_like(image_v[1])
 
@@ -181,7 +184,9 @@
 
     def add_entries(g, slot):
         rows = pl.ds(pl.multiple_of(g * 16, 16), 16)
-        total[...] += dot(by_eights(a_v[:, rows, :].astype(F32)), image_v[slot], ((1,), (1,)))
+        coeff = a_v[:, rows, :].astype(F32).reshape(n_row, per_row, 16, order)
+        coeff = jnp.transpose(coeff, (1, 0, 2, 3)).reshape(count, 16, order)
+        total[...] += dot(by_eights(coeff), image_v[slot], ((1,), (1,)))
 
     unroll = 4
 
@@ -192,7 +197,7 @@
             add_entries(jnp.maximum(g - 1, 0) if i == 0 else g - 1, (i + 1) % 2)
             image_v[i % 2] = by_eights(image)
 
-    lax.fori_loop(0, groups // unroll // 2, images, None)
+    lax.fori_loop(0, groups // unroll * 3 // 4, images, None)
 
     wait_bytes(slab_panel.at[pl.ds(0, others * TILE)], recv_sem.at[SLAB])
 
@@ -203,46 +208,49 @@
 
     lax.fori_loop(1, n_col // 2, pass_on, None)
 
-    lax.fori_loop(groups // unroll // 2, groups // unroll, images, None)
+    lax.fori_loop(groups // unroll * 3 // 4, groups // unroll, images, None)
     add_entries(groups - 1, 1)
 
-    per_row = count // n_row
     kept = jnp.where(iota((side, side), 0) % 8 == iota((side, side), 1) % 8, total[...], 0.0)
-    by_slot = jnp.sum(kept.reshape(count, 8, side), axis=1)
-    fold = jnp.where(iota((side, per_row * count), 1) % count == iota((side, per_row * count), 0) // 8, 1.0, 0.0)
-    spread = dot(by_slot, fold, precision=lax.Precision.HIGHEST)
-    spread = jnp.where(iota(spread.shape, 1) // count == iota(spread.shape, 0) % per_row, spread, 0.0)
-    pack = jnp.where(iota((n_row, count), 1) // per_row == iota((n_row, count), 0), 1.0, 0.0)
-    packed = dot(pack, spread, precision=lax.Precision.HIGHEST)
-    entry_v[...] = packed
-    gathered[pl.ds(row, 1)] = packed[None]
-
-    def to_row(k, _):
-        peer = lax.rem(row + k, n_row)
-        send(entry_v, gathered.at[row], ENTRIES, peer, col)
-
-    lax.fori_loop(1, n_row, to_row, None)
-    wait_bytes(gathered.at[pl.ds(0, n_row - 1)], recv_sem.at[ENTRIES])
-    mine = jnp.sum(jnp.where(iota(gathered.shape, 1) == row, gathered[...], 0.0), axis=1)
-    for q in range(n_row):
-        chosen[q, 0] = mine
-        chosen[q, 1] = gathered[:, q, :]
-    own_entries = pltpu.make_async_copy(chosen.at[home], entry_pairs.at[col], own_sem.at[3])
+    by_slot = jnp.concatenate(halves(jnp.sum(kept.reshape(count, 8, side), axis=1)), axis=1)
+    spread = dot(by_slot, flag(iota((2 * side, per_row * count), 1) % count == iota((2 * side, per_row * count), 0) % side // 8))
+    packed = jnp.zeros((n_row, per_row * count), F32)
+    for s4 in range(per_row):
+        mine = spread[s4 * n_row:(s4 + 1) * n_row]
+        packed += jnp.where(iota(mine.shape, 1) // count == s4, mine, 0.0)
+    for i in range(n_row):
+        same = jnp.broadcast_to(packed[i:i + 1], packed.shape)
+        chosen[i, :, 0, :] = same
+        chosen[:, i, 1, :] = same
+
+    my_block = col * n_row + row
+    own_entries = pltpu.make_async_copy(chosen.at[row, home], entry_pairs.at[my_block], own_sem.at[3])
     own_entries.start()
-    to_col(PAIRS, lambda peer: chosen.at[lax.div(peer, n_col // n_row)], entry_pairs.at[col])
+
+    def away(j):
+        return jnp.where(j < 2, j + 2, 3 - j)
+
+    def to_all(k, _):
+        y = away(lax.rem(lax.div(k, 2), 4))
+        dx = away(lax.div(k, 32)) * 2 + lax.div(y, 2)
+        dz = away(lax.rem(lax.div(k, 8), 4)) * 4 + lax.rem(y, 2) * 2 + 1 - lax.rem(k, 2)
+        r = lax.bitwise_xor(row, dx)
+        c = lax.bitwise_xor(col, dz)
+        send(chosen.at[r, lax.div(c, n_col // n_row)], entry_pairs.at[my_block], PAIRS, r, c)
+
+    every = n_row * n_col
+    lax.fori_loop(0, every - 1, to_all, None)
 
     own_slab.wait()
     wait_bytes(slab_panel.at[pl.ds(0, (others + 1) * TILE)], recv_sem.at[SLAB_PASSED])
     wait_bytes(part_panel, recv_sem.at[PART_ROWS])
-    wait_bytes(x_v.at[pl.ds(0, order - chunk)], send_sem.at[PRIMAL])
     wait_bytes(s_v.at[pl.ds(0, order - chunk)], send_sem.at[DUAL])
     wait_bytes(slab_panel.at[pl.ds(0, others * TILE)], send_sem.at[SLAB])
     wait_bytes(slab_panel.at[pl.ds(0, (others + 1) * TILE)], send_sem.at[SLAB_PASSED])
     wait_parts_sent(PART_ROWS, part_panel, part_panel.at[pl.ds(0, PW - TILE)])
-    wait_bytes(gathered.at[pl.ds(0, n_row - 1)], send_sem.at[ENTRIES])
     own_entries.wait()
-    wait_bytes(entry_pairs.at[pl.ds(0, n_col - 1)], recv_sem.at[PAIRS])
-    wait_bytes(entry_pairs.at[pl.ds(0, n_col - 1)], send_sem.at[PAIRS])
+    wait_bytes(entry_pairs.at[pl.ds(0, every - 1)], recv_sem.at[PAIRS])
+    wait_bytes(entry_pairs.at[pl.ds(0, every - 1)], send_sem.at[PAIRS])
 
 
 def finish_kernel(
@@ -289,7 +297,7 @@
         return terms[0] + terms[1]
 
     loads[1].wait()
-    own = jnp.concatenate(halves(pairs_v[:, 0].reshape(blocks, -1)), axis=1)
+    own = jnp.concatenate(halves(pairs_v[pl.ds(0, blocks, stride=2), :]), axis=1)
     for s4 in range(per_row):
         here = pl.ds(s4 * blocks, blocks)
         there = pl.ds((per_row + s4) * blocks, blocks)
@@ -301,7 +309,7 @@
         added[here, PW:] = high
         added[there, PW:] = low
 
-    other = jnp.concatenate(halves(pairs_v[:, 1].reshape(blocks, -1)), axis=1)
+    other = jnp.concatenate(halves(pairs_v[pl.ds(1, blocks, stride=2), :]), axis=1)
     loads[2].wait()
     panel = jnp.transpose(part_v[...])
     for u in range(2):
@@ -344,14 +352,14 @@
     slab, part = schur_prev.shape
     vmem = pl.BlockSpec(memory_space=pltpu.VMEM)
     hbm = pl.BlockSpec(memory_space=pltpu.HBM)
-    tile = (n_row, (count // n_row) * count)
+    lanes = (count // n_row) * count
     side = count * 8
     slab_panel, part_panel, entry_pairs, local_pos = pl.pallas_call(
         functools.partial(assemble_kernel, n_row, n_col),
         out_shape=(
             jax.ShapeDtypeStruct((PW, slab), F32),
             jax.ShapeDtypeStruct((PW, part), F32),
-            jax.ShapeDtypeStruct((n_col, 2) + tile, F32),
+            jax.ShapeDtypeStruct((blocks, 2, lanes), F32),
             jax.ShapeDtypeStruct((count, blocks), F32),
         ),
         in_specs=[hbm, hbm, hbm, vmem, vmem, hbm],
@@ -365,13 +373,12 @@
             pltpu.VMEM((TILE, slab), F32),
             pltpu.VMEM((side, side), F32),
             pltpu.VMEM((2, side, 2 * order), BF16),
-            pltpu.VMEM(tile, F32),
-            pltpu.VMEM((n_row,) + tile, F32),
-            pltpu.VMEM((n_row, 2) + tile, F32),
+            pltpu.VMEM((n_row, n_row, 2, lanes), F32),
             pltpu.SemaphoreType.DMA((4,)),
             pltpu.SemaphoreType.DMA((5,)),
-            pltpu.SemaphoreType.DMA((7,)),
-            pltpu.SemaphoreType.DMA((7,)),
+            pltpu.SemaphoreType.DMA((6,)),
+            pltpu.SemaphoreType.DMA((6,)),
+            pltpu.SemaphoreType.REGULAR,
         ],
         compiler_params=pltpu.CompilerParams(
             collective_id=0, has_side_effects=True, vmem_limit_bytes=54 * 2**20
@@ -387,7 +394,7 @@
         scratch_shapes=[
             pltpu.VMEM((PW, slab), F32),
             pltpu.VMEM((PW, part), F32),
-            pltpu.VMEM((n_col, 2) + tile, F32),
+            pltpu.VMEM((2 * blocks, lanes), F32),
             pltpu.VMEM((count, blocks), F32),
             pltpu.VMEM((PW, PW), F32),
             pltpu.VMEM((slab, part), F32),
@@ -397,7 +404,7 @@
             pltpu.SemaphoreType.DMA((2, steps)),
         ],
         compiler_params=pltpu.CompilerParams(vmem_limit_bytes=63 * 2**20),
-    )(schur_prev, slab_panel, part_panel, entry_pairs, local_pos, panel_inv)
+    )(schur_prev, slab_panel, part_panel, entry_pairs.reshape(2 * blocks, lanes), local_pos, panel_inv)
 
 
 def solution(mesh):

time: 67.6 us -> 64.1 us (0.948)
  Pallas kernels: 66.7 us -> 63.1 us
    pallas_call x1, Pallas kernels: 59.1 us -> 55.5 us  [per_device(): pl.pallas_call(functools.partial(assemble_kernel, n_row, n_col), out_shap...]
where the time goes in v3:
time: 64.1 us; the launch traced here: 63.8 us
  Pallas kernels  63.1 us (98%)
    pallas_call x1, Pallas kernels, per_device(): pl.pallas_call(functools.partial(assemble_kernel, n_row, n_col), out_shap...  55.5 us
    pallas_call x1, Pallas kernels, per_device(): pl.pallas_call(functools.partial(finish_kernel, n_row, n_col), out_shape=...  7.64 us

profile of v3, /device:TPU:1, one launch (start us, length us, event | category | flops | bytes accessed | tf_op | source)
XLA Modules:
  0.0 63.8 jit_solution(3438281892828012806)
XLA Ops:
  0.6 55.5 %shard_map.86 = (f32[256,1024]{1,0:T(8,128)}, f32[256,512]{1,0:T(8,128)}, f32[128,2,128]{2,1,0:T(2,128)}, f32[32,128]{1,0:T(8,128)}) custom-call(bf16[16,32,512]{2,1,0:T(8,128)(2,1)} %moment_x.1, bf16[16,32,512]{2,1,0:T(8,128)(2,1)} %moment_s.1, bf16[1,32,512,512]{3,2,1,0:T(8,128)(2,1)} %coeffs.1, s32[32,128]{1,0:T(8,128)} %bitcast.5, s32[64,128]{1,0:T(8,128)} %bitcast.4, ...), custom_call_target="tpu_custom_call" | custom-call | tf_op jit(solution)/shard_map/pallas_call | solution.py:357
  56.1 7.6 %shard_map.87 = (f32[1024,512]{1,0:T(8,128)}, f32[1024,256]{1,0:T(8,128)}) custom-call(f32[1024,512]{1,0:T(8,128)} %schur_prev.3, f32[256,1024]{1,0:T(8,128)} %get-tuple-element.6.slab_panel, f32[256,512]{1,0:T(8,128)} %get-tuple-element.7.part_panel, f32[256,128]{1,0:T(8,128)} %bitcast.3, f32[32,128]{1,0:T(8,128)} %get-tuple-element.9.local_pos, ...), custom_call_target="tpu_custom_call" | custom-call | tf_op jit(solution)/shard_map/pallas_call | solution.py:389

commit v4 on v3

--- a/solution.py
+++ b/solution.py
@@ -41,9 +41,9 @@
 
 def assemble_kernel(
     n_row, n_col,
-    moment_x, moment_s, coeffs, slot_con, con_pos, schur_prev,
-    slab_panel, part_panel, entry_pairs, local_pos,
-    a_v, left_v, x_v, s_v, wide_v, own_panel, total, image_v, chosen,
+    moment_x, moment_s, coeffs, slot_con, con_pos, schur_prev, panel_inv,
+    slab_factor, part_factor, entry_pairs, local_pos,
+    slab_panel, part_panel, a_v, left_v, x_v, s_v, wide_v, own_panel, total, image_v, chosen,
     a_sem, own_sem, send_sem, recv_sem, everyone,
 ):
     row = lax.axis_index("row")
@@ -74,8 +74,8 @@
     def greet(r, c):
         pl.semaphore_signal(barrier, inc=1, device_id=(r, c), device_id_type=MESH)
 
+    lax.fori_loop(1, n_row, lambda k, _: greet(lax.rem(row + k, n_row), col), None)
     lax.fori_loop(1, n_col, lambda k, _: greet(row, lax.rem(col + k, n_col)), None)
-    lax.fori_loop(1, n_row, lambda k, _: greet(lax.rem(row + k, n_row), col), None)
 
     at_home = home == row
     pl.semaphore_wait(barrier, n_col - 1 + n_row - 1)
@@ -155,10 +155,7 @@
             left_v[:, t] = dot(x_v[...], a_v[t]).astype(BF16).reshape(groups, 16, order)
 
     groups = order // 16
-    lax.fori_loop(0, a_parts, lefts, None)
-
-    own_s.wait()
-    wait_bytes(s_v.at[pl.ds(0, order - chunk)], recv_sem.at[DUAL])
+    lax.fori_loop(0, a_parts // 2, lefts, None)
     pl.semaphore_wait(everyone, n_row - 1)
 
     sibling = lax.bitwise_xor(col, 1)
@@ -173,6 +170,10 @@
     lax.fori_loop(1, n_col // 2, to_chip, None)
     to_parts(PART_ROWS, lambda half: own_panel.at[:, pl.ds(half * PART, PART)], part_panel.at[my_tile])
 
+    lax.fori_loop(a_parts // 2, a_parts, lefts, None)
+
+    own_s.wait()
+    wait_bytes(s_v.at[pl.ds(0, order - chunk)], recv_sem.at[DUAL])
     side = total.shape[0]
     per_row = count // n_row
     total[...] = jnp.zeros_like(total)
@@ -188,7 +189,7 @@
         coeff = jnp.transpose(coeff, (1, 0, 2, 3)).reshape(count, 16, order)
         total[...] += dot(by_eights(coeff), image_v[slot], ((1,), (1,)))
 
-    unroll = 4
+    unroll = 8
 
     def images(q, _):
         for i in range(unroll):
@@ -227,23 +228,31 @@
     own_entries = pltpu.make_async_copy(chosen.at[row, home], entry_pairs.at[my_block], own_sem.at[3])
     own_entries.start()
 
+    far = (2, 3, 1, 0)
+    every = n_row * n_col
+
+    def to_near(x, z, first, last):
+        for k in range(first, last):
+            y = far[k // 2]
+            r = lax.bitwise_xor(row, x * 2 + y // 2)
+            c = lax.bitwise_xor(col, z * 4 + y % 2 * 2 + 1 - k % 2)
+            send(chosen.at[r, lax.div(c, n_col // n_row)], entry_pairs.at[my_block], PAIRS, r, c)
+
     def away(j):
         return jnp.where(j < 2, j + 2, 3 - j)
 
-    def to_all(k, _):
-        y = away(lax.rem(lax.div(k, 2), 4))
-        dx = away(lax.div(k, 32)) * 2 + lax.div(y, 2)
-        dz = away(lax.rem(lax.div(k, 8), 4)) * 4 + lax.rem(y, 2) * 2 + 1 - lax.rem(k, 2)
-        r = lax.bitwise_xor(row, dx)
-        c = lax.bitwise_xor(col, dz)
-        send(chosen.at[r, lax.div(c, n_col // n_row)], entry_pairs.at[my_block], PAIRS, r, c)
-
-    every = n_row * n_col
-    lax.fori_loop(0, every - 1, to_all, None)
-
+    lax.fori_loop(0, every // 8 - 1, lambda k, _: to_near(away(lax.div(k, 4)), away(lax.rem(k, 4)), 0, 8), None)
+    to_near(0, 0, 0, 7)
+
+    inverse = halves(panel_inv[...])
+    wait_bytes(part_panel, recv_sem.at[PART_ROWS])
+    part_factor[...] = dot_halves(halves(jnp.transpose(part_panel[...])), inverse)
     own_slab.wait()
     wait_bytes(slab_panel.at[pl.ds(0, (others + 1) * TILE)], recv_sem.at[SLAB_PASSED])
-    wait_bytes(part_panel, recv_sem.at[PART_ROWS])
+    tall = slab_factor.shape[0] // 4
+    for step in range(4):
+        rows = pl.ds(step * tall, tall)
+        slab_factor[rows] = dot_halves(halves(jnp.transpose(slab_panel[:, rows])), inverse)
     wait_bytes(s_v.at[pl.ds(0, order - chunk)], send_sem.at[DUAL])
     wait_bytes(slab_panel.at[pl.ds(0, others * TILE)], send_sem.at[SLAB])
     wait_bytes(slab_panel.at[pl.ds(0, (others + 1) * TILE)], send_sem.at[SLAB_PASSED])
@@ -255,16 +264,16 @@
 
 def finish_kernel(
     n_row, n_col,
-    schur_prev, slab_panel, part_panel, entry_pairs, local_pos, panel_inv,
+    schur_prev, slab_factor, part_factor, entry_pairs, local_pos, panel_inv,
     updated, panel_factor,
-    slab_v, part_v, pairs_v, pos_v, inv_v, updated_v, factor_v, added, in_sem, out_sem,
+    part_v, pairs_v, pos_v, inv_v, updated_v, factor_v, added, at_v, at_col_v, in_sem, out_sem,
 ):
     loads = [
         pltpu.make_async_copy(src, dst, in_sem.at[k])
         for k, (src, dst) in enumerate(
             (
-                (local_pos, pos_v), (entry_pairs, pairs_v), (part_panel, part_v), (panel_inv, inv_v),
-                (slab_panel, slab_v), (schur_prev, updated_v),
+                (local_pos, pos_v), (entry_pairs, pairs_v), (panel_inv, inv_v), (part_factor, part_v),
+                (slab_factor, factor_v), (schur_prev, updated_v),
             )
         )
     ]
@@ -274,9 +283,9 @@
     col = lax.axis_index("col")
     slots, blocks = local_pos.shape
     per_row = slots // n_row
-    key = iota((2 * blocks, PW), 0) % blocks
-    tile = iota((2 * blocks, PW), 1) // TILE
-    own_key = iota((2 * blocks, PART), 0) % blocks
+    slab = schur_prev.shape[0]
+    steps = out_sem.shape[1]
+    tall = slab // steps
     loads[0].wait()
     pos = pos_v[...]
     pos16 = pos.astype(BF16)
@@ -284,56 +293,79 @@
     def slot_lanes(slot):
         return jnp.sum(jnp.where(iota(pos.shape, 0) == slot, pos, 0.0), axis=0, keepdims=True) + PART // 2
 
+    for step in range(steps):
+        half = step * tall // PART
+        within = (iota((tall, blocks), 0) + (step * tall - half * PART)).astype(F32)
+        for u in range(2):
+            hit = flag(within == slot_lanes(per_row * row + 2 * half + u))
+            at_v[step, :, u * blocks:(u + 1) * blocks] = hit
+            at_v[step, :, (2 + u) * blocks:(3 + u) * blocks] = hit
+    across = iota((PART, blocks), 0).astype(F32)
+    for u in range(2):
+        hit = flag(across == slot_lanes(2 * col + u))
+        at_col_v[:, u * blocks:(u + 1) * blocks] = hit
+        at_col_v[:, (2 + u) * blocks:(3 + u) * blocks] = hit
+
+    lanes = pairs_v.shape[1]
     in_tile, in_part = [], []
     for u in range(2):
         pick = flag(iota((slots, PW), 0) == 2 * (iota((slots, PW), 1) // TILE) + u)
         local = dot(pos16, pick, ((0,), (0,)))
         in_tile.append(local == (iota((blocks, PW), 1) % TILE - PART // 2).astype(F32))
-        local = dot(pos16, flag(iota((slots, PART), 0) == 2 * col + u), ((0,), (0,)))
+        local = jnp.tile(dot(pos16, flag(iota((slots, lanes), 0) == 2 * col + u), ((0,), (0,))), (1, PART // lanes))
         in_part.append(local == (iota((blocks, PART), 1) - PART // 2).astype(F32))
 
+    key = iota((lanes, PW), 0)
+    tile = iota((lanes, PW), 1) // TILE
+    own_key = iota((lanes, lanes), 0)
+
+    def picked(entries, pick):
+        both = dot(entries, pick)
+        return both[:blocks] + both[blocks:]
+
     def panel_terms(entries, s4):
-        terms = [jnp.where(in_tile[u], dot(entries, flag(key == s4 * slots + 2 * tile + u)), 0.0) for u in range(2)]
+        terms = [jnp.where(in_tile[u], picked(entries, flag(key == s4 * slots + 2 * tile + u)), 0.0) for u in range(2)]
         return terms[0] + terms[1]
 
+    def times_inverse(stacked):
+        return halves(dot_halves(halves(stacked), inverse))
+
+    loads[2].wait()
+    inverse = halves(inv_v[...])
     loads[1].wait()
-    own = jnp.concatenate(halves(pairs_v[pl.ds(0, blocks, stride=2), :]), axis=1)
-    for s4 in range(per_row):
-        here = pl.ds(s4 * blocks, blocks)
-        there = pl.ds((per_row + s4) * blocks, blocks)
-        high, low = halves(panel_terms(own, s4))
-        added[here, 0:PW] = high
-        added[there, 0:PW] = low
-        terms = [jnp.where(in_part[u], dot(own, flag(own_key == s4 * slots + 2 * col + u)), 0.0) for u in range(2)]
-        high, low = halves(terms[0] + terms[1])
-        added[here, PW:] = high
-        added[there, PW:] = low
-
-    other = jnp.concatenate(halves(pairs_v[pl.ds(1, blocks, stride=2), :]), axis=1)
-    loads[2].wait()
-    panel = jnp.transpose(part_v[...])
-    for u in range(2):
-        high, low = halves(panel_terms(other, 2 * lax.rem(col, n_col // n_row) + u))
-        at = flag(iota((PART, blocks), 0).astype(F32) == slot_lanes(2 * col + u))
-        panel += dot(at, high) + dot(at, low)
+    own = jnp.concatenate(halves(pairs_v[pl.ds(0, blocks, stride=2), :]), axis=0)
+    other = jnp.concatenate(halves(pairs_v[pl.ds(1, blocks, stride=2), :]), axis=0)
+    first = 2 * lax.rem(col, n_col // n_row)
+    terms = [panel_terms(other, first + u) for u in range(2)] + [panel_terms(own, s4) for s4 in range(per_row)]
+    high, low = times_inverse(jnp.concatenate(terms, axis=0))
+    deep = 2 * blocks
     loads[3].wait()
-    inverse = halves(inv_v[...])
-    columns = halves(dot_halves(halves(panel), inverse))
+    factor = part_v[...] + dot(at_col_v[...], jnp.concatenate([high[:deep], low[:deep]], axis=0))
+    columns = halves(factor)
+    for half in range(2):
+        mine = slice((half + 1) * deep, (half + 2) * deep)
+        added[half, 0:deep, 0:PW] = high[mine]
+        added[half, deep:, 0:PW] = low[mine]
+        for u in range(2):
+            s4 = 2 * half + u
+            terms = [
+                jnp.where(
+                    in_part[v],
+                    jnp.tile(picked(own, flag(own_key == s4 * slots + 2 * col + v)), (1, PART // lanes)),
+                    0.0,
+                )
+                for v in range(2)
+            ]
+            up, down = halves(terms[0] + terms[1])
+            added[half, u * blocks:(u + 1) * blocks, PW:] = up
+            added[half, (2 + u) * blocks:(3 + u) * blocks, PW:] = down
 
     loads[4].wait()
-    slab = schur_prev.shape[0]
-    steps = out_sem.shape[1]
-    tall = slab // steps
     writes = []
     for step in range(steps):
         rows = pl.ds(step * tall, tall)
-        at = []
-        for s4 in range(per_row):
-            place = slot_lanes(per_row * row + s4) + (s4 // 2) * PART
-            at.append(flag((iota((tall, blocks), 0) + step * tall).astype(F32) == place))
-        sums = dot(jnp.concatenate(at + at, axis=1), added[...])
-        panel = jnp.transpose(slab_v[:, rows]) + sums[:, :PW]
-        factor = dot_halves(halves(panel), inverse)
+        sums = dot(at_v[step], added[step * tall // PART])
+        factor = factor_v[rows] + sums[:, :PW]
         factor_v[rows] = factor
         writes.append(pltpu.make_async_copy(factor_v.at[rows], panel_factor.at[rows], out_sem.at[0, step]))
         writes[-1].start()
@@ -354,17 +386,19 @@
     hbm = pl.BlockSpec(memory_space=pltpu.HBM)
     lanes = (count // n_row) * count
     side = count * 8
-    slab_panel, part_panel, entry_pairs, local_pos = pl.pallas_call(
+    slab_factor, part_factor, entry_pairs, local_pos = pl.pallas_call(
         functools.partial(assemble_kernel, n_row, n_col),
         out_shape=(
-            jax.ShapeDtypeStruct((PW, slab), F32),
-            jax.ShapeDtypeStruct((PW, part), F32),
+            jax.ShapeDtypeStruct((slab, PW), F32),
+            jax.ShapeDtypeStruct((part, PW), F32),
             jax.ShapeDtypeStruct((blocks, 2, lanes), F32),
             jax.ShapeDtypeStruct((count, blocks), F32),
         ),
-        in_specs=[hbm, hbm, hbm, vmem, vmem, hbm],
-        out_specs=(hbm, hbm, hbm, vmem),
+        in_specs=[hbm, hbm, hbm, vmem, vmem, hbm, vmem],
+        out_specs=(vmem, vmem, hbm, vmem),
         scratch_shapes=[
+            pltpu.VMEM((PW, slab), F32),
+            pltpu.VMEM((PW, part), F32),
             pltpu.VMEM((count, order, order), BF16),
             pltpu.VMEM((order // 16, count, 16, order), BF16),
             pltpu.VMEM((order, order), BF16),
@@ -383,7 +417,7 @@
         compiler_params=pltpu.CompilerParams(
             collective_id=0, has_side_effects=True, vmem_limit_bytes=54 * 2**20
         ),
-    )(moment_x, moment_s, coeffs, slot_con.T, con_pos.reshape(-1, 128), schur_prev)
+    )(moment_x, moment_s, coeffs, slot_con.T, con_pos.reshape(-1, 128), schur_prev, panel_inv)
 
     steps = 4
     return pl.pallas_call(
@@ -392,19 +426,20 @@
         in_specs=[hbm] * 6,
         out_specs=(hbm, hbm),
         scratch_shapes=[
-            pltpu.VMEM((PW, slab), F32),
-            pltpu.VMEM((PW, part), F32),
+            pltpu.VMEM((part, PW), F32),
             pltpu.VMEM((2 * blocks, lanes), F32),
             pltpu.VMEM((count, blocks), F32),
             pltpu.VMEM((PW, PW), F32),
             pltpu.VMEM((slab, part), F32),
             pltpu.VMEM((slab, PW), F32),
-            pltpu.VMEM((2 * blocks * (count // n_row), PW + part), BF16),
+            pltpu.VMEM((2, 4 * blocks, PW + part), BF16),
+            pltpu.VMEM((steps, slab // steps, 4 * blocks), BF16),
+            pltpu.VMEM((part, 4 * blocks), BF16),
             pltpu.SemaphoreType.DMA((6,)),
             pltpu.SemaphoreType.DMA((2, steps)),
         ],
         compiler_params=pltpu.CompilerParams(vmem_limit_bytes=63 * 2**20),
-    )(schur_prev, slab_panel, part_panel, entry_pairs.reshape(2 * blocks, lanes), local_pos, panel_inv)
+    )(schur_prev, slab_factor, part_factor, entry_pairs.reshape(2 * blocks, lanes), local_pos, panel_inv)
 
 
 def solution(mesh):

time: 64.1 us -> 58.3 us (0.910)
  Pallas kernels: 63.1 us -> 57.3 us
    pallas_call x1, Pallas kernels: 55.5 us -> 51.1 us  [per_device(): pl.pallas_call(functools.partial(assemble_kernel, n_row, n_col), out_shap...]
    pallas_call x1, Pallas kernels: 7.64 us -> 6.2 us  [per_device(): pl.pallas_call(functools.partial(finish_kernel, n_row, n_col), out_shape=...]
where the time goes in v4:
time: 58.3 us; the launch traced here: 58.1 us
  Pallas kernels  57.3 us (98%)
  between operations  0.8 us (1%)
    pallas_call x1, Pallas kernels, per_device(): pl.pallas_call(functools.partial(assemble_kernel, n_row, n_col), out_shap...  51.1 us
    pallas_call x1, Pallas kernels, per_device(): pl.pallas_call(functools.partial(finish_kernel, n_row, n_col), out_shape=...  6.2 us

profile of v4, /device:TPU:1, one launch (start us, length us, event | category | flops | bytes accessed | tf_op | source)
XLA Modules:
  0.0 58.1 jit_solution(3477680738884764379)
XLA Ops:
  0.6 51.1 %shard_map.86 = (f32[1024,256]{1,0:T(8,128)}, f32[512,256]{1,0:T(8,128)}, f32[128,2,128]{2,1,0:T(2,128)}, f32[32,128]{1,0:T(8,128)}) custom-call(bf16[16,32,512]{2,1,0:T(8,128)(2,1)} %moment_x.1, bf16[16,32,512]{2,1,0:T(8,128)(2,1)} %moment_s.1, bf16[1,32,512,512]{3,2,1,0:T(8,128)(2,1)} %coeffs.1, s32[32,128]{1,0:T(8,128)} %bitcast.5, s32[64,128]{1,0:T(8,128)} %bitcast.4, ...), custom_call_target="tpu_custom_call" | custom-call | tf_op jit(solution)/shard_map/pallas_call | solution.py:389
  51.8 6.2 %shard_map.87 = (f32[1024,512]{1,0:T(8,128)}, f32[1024,256]{1,0:T(8,128)}) custom-call(f32[1024,512]{1,0:T(8,128)} %schur_prev.3, f32[1024,256]{1,0:T(8,128)} %get-tuple-element.6.slab_factor, f32[512,256]{1,0:T(8,128)} %get-tuple-element.7.part_factor, f32[256,128]{1,0:T(8,128)} %bitcast.3, f32[32,128]{1,0:T(8,128)} %get-tuple-element.9.local_pos, ...), custom_call_target="tpu_custom_call" | custom-call | tf_op jit(solution)/shard_map/pallas_call | solution.py:423

commit v5 on v4

--- a/solution.py
+++ b/solution.py
@@ -43,7 +43,7 @@
     n_row, n_col,
     moment_x, moment_s, coeffs, slot_con, con_pos, schur_prev, panel_inv,
     slab_factor, part_factor, entry_pairs, local_pos,
-    slab_panel, part_panel, a_v, left_v, x_v, s_v, wide_v, own_panel, total, image_v, chosen,
+    slab_factor_v, part_factor_v, local_pos_v, slab_panel, part_panel, a_v, left_v, x_v, s_v, wide_v, own_panel, total, image_v, chosen,
     a_sem, own_sem, send_sem, recv_sem, everyone,
 ):
     row = lax.axis_index("row")
@@ -138,8 +138,10 @@
     low_iota = iota((lanes, blocks), 0).astype(F32)
     for t in range(count):
         picked = dot(table, flag(high_iota == con_high[t:t + 1, :]), ((0,), (0,)))
-        local_pos[t:t + 1, :] = jnp.sum(jnp.where(low_iota == con_low[t:t + 1, :], picked, 0.0), axis=0, keepdims=True)
-
+        local_pos_v[t:t + 1, :] = jnp.sum(jnp.where(low_iota == con_low[t:t + 1, :], picked, 0.0), axis=0, keepdims=True)
+
+    pos_out = pltpu.make_async_copy(local_pos_v, local_pos, own_sem.at[5])
+    pos_out.start()
     wait_bytes(x_v.at[pl.ds(0, order - chunk)], send_sem.at[PRIMAL])
     to_col(DUAL, lambda peer: moment_s.at[peer], s_v.at[my_chunk])
 
@@ -246,18 +248,25 @@
 
     inverse = halves(panel_inv[...])
     wait_bytes(part_panel, recv_sem.at[PART_ROWS])
-    part_factor[...] = dot_halves(halves(jnp.transpose(part_panel[...])), inverse)
+    part_factor_v[...] = dot_halves(halves(jnp.transpose(part_panel[...])), inverse)
+    part_out = pltpu.make_async_copy(part_factor_v, part_factor, own_sem.at[6])
+    part_out.start()
     own_slab.wait()
     wait_bytes(slab_panel.at[pl.ds(0, (others + 1) * TILE)], recv_sem.at[SLAB_PASSED])
     tall = slab_factor.shape[0] // 4
     for step in range(4):
         rows = pl.ds(step * tall, tall)
-        slab_factor[rows] = dot_halves(halves(jnp.transpose(slab_panel[:, rows])), inverse)
+        slab_factor_v[rows] = dot_halves(halves(jnp.transpose(slab_panel[:, rows])), inverse)
+    slab_out = pltpu.make_async_copy(slab_factor_v, slab_factor, own_sem.at[7])
+    slab_out.start()
     wait_bytes(s_v.at[pl.ds(0, order - chunk)], send_sem.at[DUAL])
     wait_bytes(slab_panel.at[pl.ds(0, others * TILE)], send_sem.at[SLAB])
     wait_bytes(slab_panel.at[pl.ds(0, (others + 1) * TILE)], send_sem.at[SLAB_PASSED])
     wait_parts_sent(PART_ROWS, part_panel, part_panel.at[pl.ds(0, PW - TILE)])
     own_entries.wait()
+    pos_out.wait()
+    part_out.wait()
+    slab_out.wait()
     wait_bytes(entry_pairs.at[pl.ds(0, every - 1)], recv_sem.at[PAIRS])
     wait_bytes(entry_pairs.at[pl.ds(0, every - 1)], send_sem.at[PAIRS])
 
@@ -395,8 +404,11 @@
             jax.ShapeDtypeStruct((count, blocks), F32),
         ),
         in_specs=[hbm, hbm, hbm, vmem, vmem, hbm, vmem],
-        out_specs=(vmem, vmem, hbm, vmem),
+        out_specs=(hbm, hbm, hbm, hbm),
         scratch_shapes=[
+            pltpu.VMEM((slab, PW), F32),
+            pltpu.VMEM((part, PW), F32),
+            pltpu.VMEM((count, blocks), F32),
             pltpu.VMEM((PW, slab), F32),
             pltpu.VMEM((PW, part), F32),
             pltpu.VMEM((count, order, order), BF16),
@@ -409,7 +421,7 @@
             pltpu.VMEM((2, side, 2 * order), BF16),
             pltpu.VMEM((n_row, n_row, 2, lanes), F32),
             pltpu.SemaphoreType.DMA((4,)),
-            pltpu.SemaphoreType.DMA((5,)),
+            pltpu.SemaphoreType.DMA((8,)),
             pltpu.SemaphoreType.DMA((6,)),
             pltpu.SemaphoreType.DMA((6,)),
             pltpu.SemaphoreType.REGULAR,

time: 58.3 us -> 57.2 us (0.981)
  Pallas kernels: 57.3 us -> 56.2 us
    pallas_call x1, Pallas kernels: 51.1 us -> 50 us  [per_device(): pl.pallas_call(functools.partial(assemble_kernel, n_row, n_col), out_shap...]
where the time goes in v5:
time: 57.2 us; the launch traced here: 57 us
  Pallas kernels  56.2 us (98%)
  between operations  0.8 us (1%)
    pallas_call x1, Pallas kernels, per_device(): pl.pallas_call(functools.partial(assemble_kernel, n_row, n_col), out_shap...  50 us
    pallas_call x1, Pallas kernels, per_device(): pl.pallas_call(functools.partial(finish_kernel, n_row, n_col), out_shape=...  6.2 us

profile of v5, /device:TPU:1, one launch (start us, length us, event | category | flops | bytes accessed | tf_op | source)
XLA Modules:
  0.0 57.0 jit_solution(839150984864079432)
XLA Ops:
  0.6 50.0 %shard_map.86 = (f32[1024,256]{1,0:T(8,128)}, f32[512,256]{1,0:T(8,128)}, f32[128,2,128]{2,1,0:T(2,128)}, f32[32,128]{1,0:T(8,128)}) custom-call(bf16[16,32,512]{2,1,0:T(8,128)(2,1)} %moment_x.1, bf16[16,32,512]{2,1,0:T(8,128)(2,1)} %moment_s.1, bf16[1,32,512,512]{3,2,1,0:T(8,128)(2,1)} %coeffs.1, s32[32,128]{1,0:T(8,128)} %bitcast.5, s32[64,128]{1,0:T(8,128)} %bitcast.4, ...), custom_call_target="tpu_custom_call" | custom-call | tf_op jit(solution)/shard_map/pallas_call | solution.py:398
  50.6 6.2 %shard_map.87 = (f32[1024,512]{1,0:T(8,128)}, f32[1024,256]{1,0:T(8,128)}) custom-call(f32[1024,512]{1,0:T(8,128)} %schur_prev.3, f32[1024,256]{1,0:T(8,128)} %get-tuple-element.6.slab_factor, f32[512,256]{1,0:T(8,128)} %get-tuple-element.7.part_factor, f32[256,128]{1,0:T(8,128)} %bitcast.3, f32[32,128]{1,0:T(8,128)} %get-tuple-element.9.local_pos, ...), custom_call_target="tpu_custom_call" | custom-call | tf_op jit(solution)/shard_map/pallas_call | solution.py:435

commit v6 on v5

--- a/solution.py
+++ b/solution.py
@@ -170,9 +170,10 @@
         send(own_panel, slab_panel.at[my_tile], SLAB, row, lax.rem(col + 2 * k, n_col))
 
     lax.fori_loop(1, n_col // 2, to_chip, None)
+
+    lax.fori_loop(a_parts // 2, a_parts - 1, lefts, None)
     to_parts(PART_ROWS, lambda half: own_panel.at[:, pl.ds(half * PART, PART)], part_panel.at[my_tile])
-
-    lax.fori_loop(a_parts // 2, a_parts, lefts, None)
+    lax.fori_loop(a_parts - 1, a_parts, lefts, None)
 
     own_s.wait()
     wait_bytes(s_v.at[pl.ds(0, order - chunk)], recv_sem.at[DUAL])

time: 57.2 us -> 56.3 us (0.984)
  Pallas kernels: 56.2 us -> 55.3 us
    pallas_call x1, Pallas kernels: 50 us -> 49.1 us  [per_device(): pl.pallas_call(functools.partial(assemble_kernel, n_row, n_col), out_shap...]
where the time goes in v6:
time: 56.3 us; the launch traced here: 56.1 us
  Pallas kernels  55.3 us (98%)
  between operations  0.8 us (1%)
    pallas_call x1, Pallas kernels, per_device(): pl.pallas_call(functools.partial(assemble_kernel, n_row, n_col), out_shap...  49.1 us
    pallas_call x1, Pallas kernels, per_device(): pl.pallas_call(functools.partial(finish_kernel, n_row, n_col), out_shape=...  6.2 us

profile of v6, /device:TPU:1, one launch (start us, length us, event | category | flops | bytes accessed | tf_op | source)
XLA Modules:
  0.0 56.1 jit_solution(8128581003430821884)
XLA Ops:
  0.6 49.1 %shard_map.86 = (f32[1024,256]{1,0:T(8,128)}, f32[512,256]{1,0:T(8,128)}, f32[128,2,128]{2,1,0:T(2,128)}, f32[32,128]{1,0:T(8,128)}) custom-call(bf16[16,32,512]{2,1,0:T(8,128)(2,1)} %moment_x.1, bf16[16,32,512]{2,1,0:T(8,128)(2,1)} %moment_s.1, bf16[1,32,512,512]{3,2,1,0:T(8,128)(2,1)} %coeffs.1, s32[32,128]{1,0:T(8,128)} %bitcast.5, s32[64,128]{1,0:T(8,128)} %bitcast.4, ...), custom_call_target="tpu_custom_call" | custom-call | tf_op jit(solution)/shard_map/pallas_call | solution.py:399
  49.8 6.2 %shard_map.87 = (f32[1024,512]{1,0:T(8,128)}, f32[1024,256]{1,0:T(8,128)}) custom-call(f32[1024,512]{1,0:T(8,128)} %schur_prev.3, f32[1024,256]{1,0:T(8,128)} %get-tuple-element.6.slab_factor, f32[512,256]{1,0:T(8,128)} %get-tuple-element.7.part_factor, f32[256,128]{1,0:T(8,128)} %bitcast.3, f32[32,128]{1,0:T(8,128)} %get-tuple-element.9.local_pos, ...), custom_call_target="tpu_custom_call" | custom-call | tf_op jit(solution)/shard_map/pallas_call | solution.py:436
